TPU v7x, 32 devices: a whole 2x2x4 slice. The times are simulated.
32 devices in a mesh: band: 16 (over z, y, core), batch: 2 (over x).
Axes of the slice: x: 2, y: 2, z: 4, core: 2. Of those that a mesh axis runs over, the one named last changes fastest.
Arguments:
- tokens_in: bfloat16 [2, 2, 112, 112, 256], P(None, 'batch', 'band'), may hold values from -6 to 6
- cotangent: bfloat16 [2, 2, 112, 112, 256], P(None, 'batch', 'band'), may hold values from -6 to 6
- owners: int32 [4], replicated, may hold values from 0 to 31
- weight_qkv: float32 [32, 256, 768], P(('band', 'batch')), may hold values from -0.375 to 0.375
- weight_proj: float32 [32, 256, 256], P(('band', 'batch')), may hold values from -0.75 to 0.75
- weight_fc1: float32 [32, 256, 1024], P(('band', 'batch')), may hold values from -0.375 to 0.375
- weight_fc2: float32 [32, 1024, 256], P(('band', 'batch')), may hold values from -0.1875 to 0.1875
- first_qkv: float32 [32, 256, 768], P(('band', 'batch')), may hold values from -384 to 384
- second_qkv: float32 [32, 256, 768], P(('band', 'batch')), may hold values from 3010.56 to 12042.24
- first_proj: float32 [32, 256, 256], P(('band', 'batch')), may hold values from -384 to 384
- second_proj: float32 [32, 256, 256], P(('band', 'batch')), may hold values from 3010.56 to 12042.24
- first_fc1: float32 [32, 256, 1024], P(('band', 'batch')), may hold values from -384 to 384
- second_fc1: float32 [32, 256, 1024], P(('band', 'batch')), may hold values from 3010.56 to 12042.24
- first_fc2: float32 [32, 1024, 256], P(('band', 'batch')), may hold values from -384 to 384
- second_fc2: float32 [32, 1024, 256], P(('band', 'batch')), may hold values from 3010.56 to 12042.24
- left_qkv: float32 [256, 256], replicated, may hold values from -1 to 1, as said below
- right_qkv: float32 [768, 768], replicated, may hold values from -1 to 1, as said below
- left_proj: float32 [256, 256], replicated, may hold values from -1 to 1, as said below
- right_proj: float32 [256, 256], replicated, may hold values from -1 to 1, as said below
- left_fc1: float32 [256, 256], replicated, may hold values from -1 to 1, as said below
- right_fc1: float32 [1024, 1024], replicated, may hold values from -1 to 1, as said below
- left_fc2: float32 [1024, 1024], replicated, may hold values from -1 to 1, as said below
- right_fc2: float32 [256, 256], replicated, may hold values from -1 to 1, as said below
- vectors: float32 [22, 256], replicated, may hold values from -0.5 to 1.5, as said below
- vectors_first: float32 [22, 256], replicated, may hold values from -384 to 384
- vectors_second: float32 [22, 256], replicated, may hold values from 3010.56 to 12042.24
Outputs:
- block_out: bfloat16 [2, 2, 112, 112, 256], P(None, 'batch', 'band')
- input_grad: bfloat16 [2, 2, 112, 112, 256], P(None, 'batch', 'band')
- grad_qkv: float32 [256, 768], replicated
- first_new_qkv: float32 [32, 256, 768], P(('band', 'batch'))
- second_new_qkv: float32 [32, 256, 768], P(('band', 'batch'))
- weight_new_qkv: float32 [32, 256, 768], P(('band', 'batch'))
- grad_proj: float32 [256, 256], replicated
- first_new_proj: float32 [32, 256, 256], P(('band', 'batch'))
- second_new_proj: float32 [32, 256, 256], P(('band', 'batch'))
- weight_new_proj: float32 [32, 256, 256], P(('band', 'batch'))
- grad_fc1: float32 [256, 1024], replicated
- first_new_fc1: float32 [32, 256, 1024], P(('band', 'batch'))
- second_new_fc1: float32 [32, 256, 1024], P(('band', 'batch'))
- weight_new_fc1: float32 [32, 256, 1024], P(('band', 'batch'))
- grad_fc2: float32 [1024, 256], replicated
- first_new_fc2: float32 [32, 1024, 256], P(('band', 'batch'))
- second_new_fc2: float32 [32, 1024, 256], P(('band', 'batch'))
- weight_new_fc2: float32 [32, 1024, 256], P(('band', 'batch'))
- vectors_grad: float32 [22, 256], replicated
- vectors_first_new: float32 [22, 256], replicated
- vectors_second_new: float32 [22, 256], replicated
- vectors_new: float32 [22, 256], replicated
Inputs may be any that keep to these rules, and one draw needn't show every extreme that they name: `left_qkv`: an orthogonal 256 x 256 matrix. `right_qkv`: an orthogonal 3 * 256 x 3 * 256 matrix. `left_proj`: an orthogonal 256 x 256 matrix. `right_proj`: an orthogonal 256 x 256 matrix. `left_fc1`: an orthogonal 256 x 256 matrix. `right_fc1`: an orthogonal 1024 x 1024 matrix. `left_fc2`: an orthogonal 1024 x 1024 matrix. `right_fc2`: an orthogonal 256 x 256 matrix. `vectors`: gains in rows 0 and 5 from 0.5 to 1.5, taps from -0.5 to 0.5, biases from -0.2 to 0.2.
All inputs are finite; a program needn't handle non-finite values.
Results may differ from a plain program's by a relative error of at most 0.011.
Values may be sent and summed in bfloat16 or wider, within the bound.
A program may use at most 512 MiB of HBM per device.

v0:
```python
import jax
import jax.numpy as jnp
from jax import lax
from jax.sharding import PartitionSpec as P

HEAD_DIM = 32
STEP = 10


EPS_NORM = 1e-05
BETA_ONE = 0.5
BETA_TWO = 0.6
RATE = 0.04
RATE_VECTORS = 0.2
DECAY = 0.01
EPS_ADAM = 1e-08
HIGH = lax.Precision.HIGHEST


def exact_gelu(values):
    return jax.nn.gelu(values, approximate=False)


def layer_stats(values):
    row_mean = jnp.mean(values, axis=-1, keepdims=True)
    centred = values - row_mean
    inverse = lax.rsqrt(jnp.mean(centred * centred, axis=-1, keepdims=True) + EPS_NORM)
    return (centred * inverse, inverse)


def norm_back(grad_normed, gain_vec, unit_rows, inverse):
    scaled = grad_normed * gain_vec
    first_mean = jnp.mean(scaled, axis=-1, keepdims=True)
    second_mean = jnp.mean(scaled * unit_rows, axis=-1, keepdims=True)
    return inverse * (scaled - first_mean - unit_rows * second_mean)


def position_conv(values, tap_weights, tap_shift, rows_n, cols_n):
    grid_view = values.reshape(values.shape[0], rows_n, cols_n, values.shape[-1])
    padded = jnp.pad(grid_view, ((0, 0), (1, 1), (1, 1), (0, 0)))
    summed = jnp.zeros_like(grid_view) + tap_shift
    for tap_index in range(9):
        row_off = tap_index // 3
        col_off = tap_index % 3
        summed = (
            summed
            + padded[:, row_off : row_off + rows_n, col_off : col_off + cols_n, :]
            * tap_weights[tap_index]
        )
    return summed.reshape(values.shape)


def split_window(window):
    part_width = window.shape[-1] // 3
    tokens_n = window.shape[0]
    head_count = part_width // HEAD_DIM
    query_h = window[:, :part_width].reshape(tokens_n, head_count, HEAD_DIM)
    key_h = window[:, part_width : 2 * part_width].reshape(tokens_n, head_count, HEAD_DIM)
    value_h = window[:, 2 * part_width :].reshape(tokens_n, head_count, HEAD_DIM)
    return (query_h, key_h, value_h)


def attend_forward(window):
    query_h, key_h, value_h = split_window(window)
    scores = jnp.einsum(
        "qhd,khd->hqk", query_h, key_h, preferred_element_type=jnp.float32
    ) * HEAD_DIM ** (-0.5)
    highest = jnp.max(scores, axis=-1, keepdims=True)
    expo_s = jnp.exp(scores - highest)
    row_total = jnp.sum(expo_s, axis=-1, keepdims=True)
    softmax_p = (expo_s / row_total).astype(jnp.bfloat16)
    attended = jnp.einsum("hqk,khd->qhd", softmax_p, value_h, preferred_element_type=jnp.float32)
    return (attended.reshape(window.shape[0], window.shape[-1] // 3), highest + jnp.log(row_total))


def attend_backward(pieces):
    window, log_total, grad_out = pieces
    query_h, key_h, value_h = split_window(window)
    scale_q = HEAD_DIM ** (-0.5)
    scores = (
        jnp.einsum("qhd,khd->hqk", query_h, key_h, preferred_element_type=jnp.float32) * scale_q
    )
    softmax_f = jnp.exp(scores - log_total)
    grad_h = grad_out.reshape(query_h.shape)
    grad_value = jnp.einsum(
        "hqk,qhd->khd", softmax_f.astype(jnp.bfloat16), grad_h, preferred_element_type=jnp.float32
    )
    grad_soft = jnp.einsum("qhd,khd->hqk", grad_h, value_h, preferred_element_type=jnp.float32)
    inner_sum = jnp.sum(softmax_f * grad_soft, axis=-1, keepdims=True)
    grad_scores = (softmax_f * (grad_soft - inner_sum)).astype(jnp.bfloat16)
    grad_query = (
        jnp.einsum("hqk,khd->qhd", grad_scores, key_h, preferred_element_type=jnp.float32) * scale_q
    )
    grad_key = (
        jnp.einsum("hqk,qhd->khd", grad_scores, query_h, preferred_element_type=jnp.float32)
        * scale_q
    )
    tokens_n = window.shape[0]
    part_width = window.shape[-1] // 3
    return jnp.concatenate(
        [
            grad_query.reshape(tokens_n, part_width),
            grad_key.reshape(tokens_n, part_width),
            grad_value.reshape(tokens_n, part_width),
        ],
        axis=-1,
    )


def window_forward(packed, tap_weights, tap_shift, rows_n, cols_n):
    part_width = packed.shape[-1] // 3
    attended, log_total = lax.map(attend_forward, packed)
    conv_out = position_conv(
        packed[..., 2 * part_width :].astype(jnp.float32), tap_weights, tap_shift, rows_n, cols_n
    )
    return (attended + conv_out, log_total)


def window_backward(packed, log_total, grad_out, tap_weights, tap_shift, rows_n, cols_n):
    part_width = packed.shape[-1] // 3
    grad_parts = lax.map(attend_backward, (packed, log_total, grad_out))

    def conv_part(values, taps_in, shift_in):
        return position_conv(values, taps_in, shift_in, rows_n, cols_n)

    conv_value, conv_pull = jax.vjp(
        conv_part, packed[..., 2 * part_width :].astype(jnp.float32), tap_weights, tap_shift
    )
    grad_conv, grad_taps, grad_shift = conv_pull(grad_out.astype(jnp.float32))
    grad_total = jnp.concatenate(
        [grad_parts[..., : 2 * part_width], grad_parts[..., 2 * part_width :] + grad_conv], axis=-1
    )
    return (grad_total.astype(jnp.bfloat16), grad_taps, grad_shift)


def rotated_adam(packed):
    grad, first, second, weight, left_basis, right_basis = packed
    turned = jnp.dot(jnp.dot(left_basis.T, grad, precision=HIGH), right_basis, precision=HIGH)
    first_new = BETA_ONE * first + (1.0 - BETA_ONE) * turned
    second_new = BETA_TWO * second + (1.0 - BETA_TWO) * turned * turned
    direction = (
        first_new
        / (1.0 - BETA_ONE**STEP)
        / (jnp.sqrt(second_new / (1.0 - BETA_TWO**STEP)) + EPS_ADAM)
    )
    back_turned = jnp.dot(
        jnp.dot(left_basis, direction, precision=HIGH), right_basis.T, precision=HIGH
    )
    weight_new = weight - RATE * back_turned - RATE * DECAY * weight
    return (first_new, second_new, weight_new)


def skipped_step(packed):
    return (jnp.zeros_like(packed[1]), jnp.zeros_like(packed[2]), jnp.zeros_like(packed[3]))


def own_slot(slot, owner_id, device_index):
    return jnp.where(device_index == owner_id, slot[0], 0.0)


def per_device(
    tokens_in,
    cotangent,
    owners,
    weight_qkv,
    weight_proj,
    weight_fc1,
    weight_fc2,
    first_qkv,
    second_qkv,
    first_proj,
    second_proj,
    first_fc1,
    second_fc1,
    first_fc2,
    second_fc2,
    left_qkv,
    right_qkv,
    left_proj,
    right_proj,
    left_fc1,
    right_fc1,
    left_fc2,
    right_fc2,
    vectors,
    vectors_first,
    vectors_second,
):
    device_index = lax.axis_index(("band", "batch"))
    gathered = lax.psum(
        (
            own_slot(weight_qkv, owners[0], device_index),
            own_slot(weight_proj, owners[1], device_index),
            own_slot(weight_fc1, owners[2], device_index),
            own_slot(weight_fc2, owners[3], device_index),
        ),
        ("band", "batch"),
    )
    qkv_low = gathered[0].astype(jnp.bfloat16)
    proj_low = gathered[1].astype(jnp.bfloat16)
    fc1_low = gathered[2].astype(jnp.bfloat16)
    fc2_low = gathered[3].astype(jnp.bfloat16)
    micro_n, images_n, band_rows, cols_all, channels = tokens_in.shape
    half_width = channels // 2
    bias_qkv = jnp.concatenate([vectors[2], jnp.zeros_like(vectors[2]), vectors[3]])
    tap_weights = vectors[12:21]
    tap_shift = vectors[21]
    outputs_list = []
    input_grads = []
    totals = None
    for micro_step in range(micro_n):
        tokens_f = tokens_in[micro_step].astype(jnp.float32).reshape(-1, channels)
        unit_one, inverse_one = layer_stats(tokens_f)
        normed_one = (unit_one * vectors[0] + vectors[1]).astype(jnp.bfloat16)
        qkv_act = (
            jnp.dot(normed_one, qkv_low, preferred_element_type=jnp.float32) + bias_qkv
        ).astype(jnp.bfloat16)
        qkv_grid = qkv_act.reshape(images_n, band_rows, cols_all, 3 * channels)
        horizontal_in = jnp.concatenate(
            [qkv_grid[..., block * channels : block * channels + half_width] for block in range(3)],
            axis=-1,
        )
        vertical_in = jnp.concatenate(
            [
                qkv_grid[..., block * channels + half_width : (block + 1) * channels]
                for block in range(3)
            ],
            axis=-1,
        )
        columns = lax.all_to_all(vertical_in, "band", split_axis=2, concat_axis=1, tiled=True)
        rows_all = columns.shape[1]
        stripe_cols = columns.shape[2]
        columns_flat = columns.reshape(images_n, rows_all * stripe_cols, 3 * half_width)
        horizontal_flat = horizontal_in.reshape(images_n, band_rows * cols_all, 3 * half_width)
        horiz_out, horiz_log = window_forward(
            horizontal_flat,
            tap_weights[:, :half_width],
            tap_shift[:half_width],
            band_rows,
            cols_all,
        )
        vert_out, vert_log = window_forward(
            columns_flat, tap_weights[:, half_width:], tap_shift[half_width:], rows_all, stripe_cols
        )
        vert_rows = lax.all_to_all(
            vert_out.astype(jnp.bfloat16).reshape(images_n, rows_all, stripe_cols, half_width),
            "band",
            split_axis=1,
            concat_axis=2,
            tiled=True,
        )
        joined = jnp.concatenate(
            [
                horiz_out.astype(jnp.bfloat16).reshape(images_n, band_rows, cols_all, half_width),
                vert_rows,
            ],
            axis=-1,
        ).reshape(-1, channels)
        middle = (
            tokens_f + jnp.dot(joined, proj_low, preferred_element_type=jnp.float32) + vectors[4]
        )
        unit_two, inverse_two = layer_stats(middle)
        normed_two = (unit_two * vectors[5] + vectors[6]).astype(jnp.bfloat16)
        hidden = jnp.dot(normed_two, fc1_low, preferred_element_type=jnp.float32) + vectors[
            7:11
        ].reshape(-1)
        active, gelu_pull = jax.vjp(exact_gelu, hidden)
        active_low = active.astype(jnp.bfloat16)
        block_rows = (
            middle + jnp.dot(active_low, fc2_low, preferred_element_type=jnp.float32) + vectors[11]
        )
        outputs_list.append(block_rows.astype(jnp.bfloat16).reshape(tokens_in.shape[1:]))
        grad_top = cotangent[micro_step].reshape(-1, channels)
        grad_f = grad_top.astype(jnp.float32)
        grad_wfc2 = jnp.dot(active_low.T, grad_top, preferred_element_type=jnp.float32)
        grad_active = jnp.dot(grad_top, fc2_low.T, preferred_element_type=jnp.float32)
        grad_hidden = gelu_pull(grad_active)[0].astype(jnp.bfloat16)
        grad_wfc1 = jnp.dot(normed_two.T, grad_hidden, preferred_element_type=jnp.float32)
        grad_normed_two = jnp.dot(grad_hidden, fc1_low.T, preferred_element_type=jnp.float32)
        grad_middle = grad_f + norm_back(grad_normed_two, vectors[5], unit_two, inverse_two)
        grad_branch = grad_middle.astype(jnp.bfloat16)
        grad_wproj = jnp.dot(joined.T, grad_branch, preferred_element_type=jnp.float32)
        grad_joined = jnp.dot(grad_branch, proj_low.T, preferred_element_type=jnp.float32).astype(
            jnp.bfloat16
        )
        grad_joined = grad_joined.reshape(images_n, band_rows, cols_all, channels)
        grad_horiz, horiz_taps, horiz_shift = window_backward(
            horizontal_flat,
            horiz_log,
            grad_joined[..., :half_width].reshape(images_n, -1, half_width),
            tap_weights[:, :half_width],
            tap_shift[:half_width],
            band_rows,
            cols_all,
        )
        grad_columns = lax.all_to_all(
            grad_joined[..., half_width:], "band", split_axis=2, concat_axis=1, tiled=True
        )
        grad_vert, vert_taps, vert_shift = window_backward(
            columns_flat,
            vert_log,
            grad_columns.reshape(images_n, -1, half_width),
            tap_weights[:, half_width:],
            tap_shift[half_width:],
            rows_all,
            stripe_cols,
        )
        grad_vert_rows = lax.all_to_all(
            grad_vert.reshape(images_n, rows_all, stripe_cols, 3 * half_width),
            "band",
            split_axis=1,
            concat_axis=2,
            tiled=True,
        )
        grad_horiz_grid = grad_horiz.reshape(images_n, band_rows, cols_all, 3 * half_width)
        pieces_list = []
        for block in range(3):
            pieces_list.append(grad_horiz_grid[..., block * half_width : (block + 1) * half_width])
            pieces_list.append(grad_vert_rows[..., block * half_width : (block + 1) * half_width])
        grad_qkv_act = jnp.concatenate(pieces_list, axis=-1).reshape(-1, 3 * channels)
        grad_wqkv = jnp.dot(normed_one.T, grad_qkv_act, preferred_element_type=jnp.float32)
        grad_normed_one = jnp.dot(grad_qkv_act, qkv_low.T, preferred_element_type=jnp.float32)
        grad_input = grad_middle + norm_back(grad_normed_one, vectors[0], unit_one, inverse_one)
        input_grads.append(grad_input.astype(jnp.bfloat16).reshape(tokens_in.shape[1:]))
        qkv_sums = jnp.sum(grad_qkv_act.astype(jnp.float32), axis=0)
        hidden_sums = jnp.sum(grad_hidden.astype(jnp.float32), axis=0)
        grad_vectors = jnp.concatenate(
            [
                jnp.sum(grad_normed_one * unit_one, axis=0)[None],
                jnp.sum(grad_normed_one, axis=0)[None],
                qkv_sums[:channels][None],
                qkv_sums[2 * channels :][None],
                jnp.sum(grad_branch.astype(jnp.float32), axis=0)[None],
                jnp.sum(grad_normed_two * unit_two, axis=0)[None],
                jnp.sum(grad_normed_two, axis=0)[None],
                hidden_sums.reshape(-1, channels),
                jnp.sum(grad_f, axis=0)[None],
                jnp.concatenate([horiz_taps, vert_taps], axis=-1),
                jnp.concatenate([horiz_shift, vert_shift], axis=-1)[None],
            ],
            axis=0,
        )
        local_grads = (grad_wqkv, grad_wproj, grad_wfc1, grad_wfc2, grad_vectors)
        if totals is None:
            totals = local_grads
        else:
            totals = jax.tree.map(jnp.add, totals, local_grads)
    totals = lax.psum((totals[0], totals[1], totals[2], totals[3], totals[4]), ("band", "batch"))
    block_out = jnp.stack(outputs_list, axis=0)
    input_grad = jnp.stack(input_grads, axis=0)
    results = [block_out, input_grad]
    plan = (
        (totals[0], 0, first_qkv, second_qkv, weight_qkv, left_qkv, right_qkv),
        (totals[1], 1, first_proj, second_proj, weight_proj, left_proj, right_proj),
        (totals[2], 2, first_fc1, second_fc1, weight_fc1, left_fc1, right_fc1),
        (totals[3], 3, first_fc2, second_fc2, weight_fc2, left_fc2, right_fc2),
    )
    for grad, which, first_slot, second_slot, weight_slot, left_basis, right_basis in plan:
        is_owner = device_index == owners[which]
        first_new, second_new, weight_new = lax.cond(
            is_owner,
            rotated_adam,
            skipped_step,
            (grad, first_slot[0], second_slot[0], weight_slot[0], left_basis, right_basis),
        )
        results.append(grad)
        results.append(first_new[None])
        results.append(second_new[None])
        results.append(weight_new[None])
    vectors_grad = totals[4]
    vec_first_new = BETA_ONE * vectors_first + (1.0 - BETA_ONE) * vectors_grad
    vec_second_new = BETA_TWO * vectors_second + (1.0 - BETA_TWO) * vectors_grad * vectors_grad
    vec_step = (
        vec_first_new
        / (1.0 - BETA_ONE**STEP)
        / (jnp.sqrt(vec_second_new / (1.0 - BETA_TWO**STEP)) + EPS_ADAM)
    )
    vectors_new = vectors - RATE_VECTORS * vec_step
    return (
        results[0],
        results[1],
        results[2],
        results[3],
        results[4],
        results[5],
        results[6],
        results[7],
        results[8],
        results[9],
        results[10],
        results[11],
        results[12],
        results[13],
        results[14],
        results[15],
        results[16],
        results[17],
        vectors_grad,
        vec_first_new,
        vec_second_new,
        vectors_new,
    )


def solution(mesh):
    return jax.shard_map(
        per_device,
        mesh=mesh,
        in_specs=(
            P(None, "batch", "band", None, None),
            P(None, "batch", "band", None, None),
            P(),
            P(("band", "batch"), None, None),
            P(("band", "batch"), None, None),
            P(("band", "batch"), None, None),
            P(("band", "batch"), None, None),
            P(("band", "batch"), None, None),
            P(("band", "batch"), None, None),
            P(("band", "batch"), None, None),
            P(("band", "batch"), None, None),
            P(("band", "batch"), None, None),
            P(("band", "batch"), None, None),
            P(("band", "batch"), None, None),
            P(("band", "batch"), None, None),
            P(),
            P(),
            P(),
            P(),
            P(),
            P(),
            P(),
            P(),
            P(),
            P(),
            P(),
        ),
        out_specs=(
            P(None, "batch", "band", None, None),
            P(None, "batch", "band", None, None),
            P(),
            P(("band", "batch"), None, None),
            P(("band", "batch"), None, None),
            P(("band", "batch"), None, None),
            P(),
            P(("band", "batch"), None, None),
            P(("band", "batch"), None, None),
            P(("band", "batch"), None, None),
            P(),
            P(("band", "batch"), None, None),
            P(("band", "batch"), None, None),
            P(("band", "batch"), None, None),
            P(),
            P(("band", "batch"), None, None),
            P(("band", "batch"), None, None),
            P(("band", "batch"), None, None),
            P(),
            P(),
            P(),
            P(),
        ),
        check_vma=False,
    )
```

profile of v0, /device:TPU:0, one launch (start us, length us, event | category | flops | bytes accessed | tf_op | source)
XLA Modules:
  0.0 745.8 jit_solution(5042633712178352855)
XLA Ops:
  21.9 80.7 %all-reduce.82 = (bf16[256,256]{1,0:T(8,128)(2,1)S(1)}, bf16[256,768]{1,0:T(8,128)(2,1)}, bf16[256,1024]{1,0:T(8,128)(2,1)}, bf16[1024,256]{1,0:T(8,128)(2,1)}) all-reduce(f32[256,256]{1,0:T(8,128)S(1)} %broadcast_select_fusion.3, f32[256,768]{1,0:T(8,128)} %broadcast_select_fusion.2, ...), channel_id=1, replica_groups=mesh['band'=16,'batch'=2] {'band','batch'}, use_global_device_ids=true, to_apply=%region_7.8 | all-reduce | flops 786432 | bytes 4718592 | tf_op jit(solution)/shard_map/psum | solution.py:190
  107.2 4.5 all-to-all-start
  128.5 3.1 fusion.133
  138.7 2.8 fusion.135
  143.3 5.0 add_convert_fusion.11
  154.8 6.1 all-to-all-start.2
  169.4 8.6 %all-to-all-done.2 = bf16[1,7,112,384]{3,1,0,2:T(8,128)(2,1)S(1)} async-done(((bf16[1,7,112,384]{3,1,0,2:T(8,128)(2,1)}), bf16[1,7,112,384]{3,1,0,2:T(8,128)(2,1)S(1)}, u32[]{:S(2)}, u32[]{:S(2)}) %all-to-all-start.2) | async-done | bytes 602144 | tf_op jit(solution)/shard_map/all_to_all | solution.py:230
  190.7 3.1 fusion.132
  197.6 2.6 multiply_reduce_fusion.6
  204.4 3.1 fusion.134
  211.2 3.5 fusion.163
  215.5 4.9 all-to-all-start.1
  221.2 8.7 %all-to-all-done.1 = bf16[1,112,7,128]{3,2,0,1:T(8,128)(2,1)S(1)} async-done(((bf16[1,112,7,128]{3,2,0,1:T(8,128)(2,1)}), bf16[1,112,7,128]{3,2,0,1:T(8,128)(2,1)S(1)}, u32[]{:S(2)}, u32[]{:S(2)}) %all-to-all-start.1) | async-done | bytes 200736 | tf_op jit(solution)/shard_map/all_to_all | solution.py:245
  229.9 4.4 all-to-all-start.3
  237.5 6.4 all-to-all-done.3
  249.9 16.0 %multiply_convert_fusion.5 = (bf16[784,1024]{1,0:T(8,128)(2,1)}, f32[784,1024]{1,0:T(8,128)S(1)}, bf16[784,1024]{1,0:T(8,128)(2,1)}, f32[784,1024]{1,0:T(8,128)S(1)}, f32[784,1024]{1,0:T(8,128)S(1)}) fusion(f32[1024]{0:T(1024)S(1)} %bitcast.645, f32[784,1024]{1,0:T(8,128)S(1)} %fusion.192, bf16[256,1024]{1,0:T(8,128)(2,1)S(1)} %copy-done.49, ...), kind=kOutput, calls=%fused_computation.169 | convolution fusion | flops 518017024 | bytes 17395840 | tf_op jit(solution)/shard_map/dot_general | solution.py:264
  279.7 6.9 fusion.140
  286.6 2.7 convert_reduce_fusion.7
  295.0 7.3 fusion.149
  302.3 6.9 fusion.90
  309.3 5.4 multiply_reduce_fusion.1
  314.6 6.9 multiply_convert_fusion.1
  327.7 2.9 multiply_reduce_fusion.3
  330.6 2.6 multiply_convert_fusion.3
  344.4 3.5 all-to-all-start.6
  353.1 3.4 pad_add_fusion.10
  360.4 3.4 pad_add_fusion.4
  380.9 3.4 convolution_add_fusion.1
  384.3 6.2 all-to-all-start.4
  391.9 6.9 fusion.88
  398.8 5.8 multiply_reduce_fusion
  404.7 2.6 multiply_convert_fusion
  413.0 6.8 fusion.92
  419.8 8.4 %multiply_reduce_fusion.2 = (f32[4,784]{1,0:T(4,128)S(1)}, f32[4,784,784]{1,2,0:T(8,128)}) fusion(f32[4,784,784]{1,2,0:T(8,128)} %copy-done, f32[4,784]{1,0:T(4,128)S(1)} %log_add_fusion.2, bf16[784,4,32]{0,2,1:T(8,128)(2,1)S(1)} %copy.405, bf16[784,4,32]{0,2,1:T(8,128)(2,1)S(1)} %bitcast.601), kind=kOutput, calls=%fused_computation.99 | convolution fusion | flops 167183296 | bytes 20095488 | tf_op jit(solution)/shard_map/while/body/eval_jaxpr/qhd,khd->hqk/dot_general | solution.py:88
  442.8 6.3 all-to-all-start.7
  449.1 8.6 %multiply_convert_fusion.2 = bf16[4,784,784]{1,2,0:T(8,128)(2,1)S(1)} fusion(f32[4,784,784]{1,2,0:T(8,128)} %get-tuple-element.504, f32[4,784,784]{1,2,0:T(8,128)} %copy-done, f32[4,784]{1,0:T(4,128)S(1)} %get-tuple-element.503, f32[4,784]{1,0:T(4,128)S(1)} %log_add_fusion.2), kind=kLoop, calls=%fused_computation.98 | loop fusion | flops 12293120 | bytes 24611328 | tf_op jit(solution)/shard_map/while/body/eval_jaxpr/convert_element_type | solution.py:90
  466.7 4.3 convolution_multiply_fusion.8
  474.0 2.9 fusion.168
  478.6 2.8 fusion.137
  484.5 6.1 all-to-all-start.5
  497.3 10.5 %all-to-all-done.5 = bf16[1,112,7,384]{3,2,0,1:T(8,128)(2,1)} async-done(((bf16[1,112,7,384]{3,2,0,1:T(8,128)(2,1)}), bf16[1,112,7,384]{3,2,0,1:T(8,128)(2,1)}, u32[]{:S(2)}, u32[]{:S(2)}) %all-to-all-start.5) | async-done | bytes 602144 | tf_op jit(solution)/shard_map/all_to_all | solution.py:308
  522.9 2.8 fusion.221
  528.3 40.2 %psum.71 = f32[22,256]{1,0:T(8,128)S(1)} all-reduce(f32[22,256]{1,0:T(8,128)S(1)} %add.714), channel_id=1, replica_groups=mesh['band'=16,'batch'=2] {'band','batch'}, use_global_device_ids=true, to_apply=%region_100.101 | all-reduce | flops 5632 | bytes 45056 | tf_op jit(solution)/shard_map/psum | solution.py:348
  568.6 3.1 convolution_add_fusion.6
  575.6 134.8 %all-reduce.81.cloned.1.call-done = (f32[256,768]{1,0:T(8,128)}, f32[256,256]{1,0:T(8,128)}, f32[256,1024]{1,0:T(8,128)}, f32[1024,256]{1,0:T(8,128)}) async-done(((f32[256,768]{1,0:T(8,128)}, f32[256,256]{1,0:T(8,128)}, f32[256,1024]{1,0:T(8,128)}, f32[1024,256]{1,0:T(8,128)}), (f32[256,768]{1,0:T(8,128)}, f32[256,256]{1,0:T(8,128)}, f32[256,1024]{1,0:T(8,128)}, ...) | async-done | bytes 3145744 | tf_op jit(solution)/shard_map/psum | solution.py:348
  713.1 19.9 %conditional.7 = (f32[1,1024,256]{2,1,0:T(8,128)S(1)}, f32[1,1024,256]{2,1,0:T(8,128)S(1)}, f32[1,1024,256]{2,1,0:T(8,128)S(1)}) conditional(s32[]{:T(128)} %convert_element_type.563, () %tuple.86, (f32[1024,1024]{1,0:T(8,128)}, f32[1024,256]{1,0:T(8,128)}, f32[256,256]{1,0:T(8,128)}, f32[1,1024,256]{2,1,0:T(8,128)}, f32[1,1024,256]{2,1,0:T(8,128)}, ...), branch_computations={%region_42.43_spmd, %region_43.44_spmd} | conditional | flops 8058044416 | bytes 51904648 | solution.py:360
  713.1 8.9 %fusion.218 = f32[1024,256]{1,0:T(8,128)S(1)} fusion(f32[1024,1024]{1,0:T(8,128)} %get-tuple-element.272, f32[1024,256]{1,0:T(8,128)} %get-tuple-element.182), kind=kOutput, calls=%fused_computation.572 | convolution fusion | flops 3221225472 | bytes 6291456 | tf_op jit(solution)/shard_map/cond/branch_1_fun/dot_general | solution.py:138
  723.1 7.5 %fusion.64 = f32[256,1024]{1,0:T(8,128)S(1)} fusion(f32[1024,1024]{1,0:T(8,128)S(1)} %copy-done.10, f32[1024,256]{1,0:T(8,128)S(1)} %fusion.219, f32[1,1024,256]{2,1,0:T(8,128)S(1)} %copy-done.27, f32[1,1024,256]{2,1,0:T(8,128)S(1)} %copy-done.28), kind=kOutput, calls=%fused_computation.76 | convolution fusion | flops 3223584768 | bytes 8388608 | tf_op jit(solution)/shard_map/cond/branch_1_fun/dot_general | solution.py:147
  (738 shorter events, 231.3 us)
Async XLA Ops:
  7.2 13.6 %copy-start.22 = (f32[1,256,1024]{2,1,0:T(8,128)S(1)}, f32[1,256,1024]{2,1,0:T(8,128)}, u32[]{:S(2)}) copy-start(f32[1,256,1024]{2,1,0:T(8,128)} %param.39) | copy-start | bytes 3145732
  8.8 93.8 %copy-start.141 = (f32[784]{0:T(1024)}, f32[784]{0:T(1024)S(1)}, u32[]{:S(2)}) copy-start(f32[784]{0:T(1024)S(1)} %div.169) | copy-start | bytes 9412
  8.9 93.7 %copy-start.143 = (f32[784]{0:T(1024)}, f32[784]{0:T(1024)S(1)}, u32[]{:S(2)}) copy-start(f32[784]{0:T(1024)S(1)} %div.160) | copy-start | bytes 9412
  16.1 97.8 %copy-start.154 = (f32[1,256]{1,0:T(1,128)}, f32[1,256]{1,0:T(1,128)S(1)}, u32[]{:S(2)}) copy-start(f32[1,256]{1,0:T(1,128)S(1)} %get-tuple-element.448) | copy-start | bytes 3076
  16.1 97.8 %copy-start.198 = (f32[1,256]{1,0:T(1,128)}, f32[1,256]{1,0:T(1,128)S(1)}, u32[]{:S(2)}) copy-start(f32[1,256]{1,0:T(1,128)S(1)} %get-tuple-element.447) | copy-start | bytes 3076
  16.2 86.4 %copy-start.145 = (f32[784]{0:T(1024)}, f32[784]{0:T(1024)S(1)}, u32[]{:S(2)}) copy-start(f32[784]{0:T(1024)S(1)} %rsqrt.41) | copy-start | bytes 9412
  16.3 86.3 %copy-start.147 = (f32[784]{0:T(1024)}, f32[784]{0:T(1024)S(1)}, u32[]{:S(2)}) copy-start(f32[784]{0:T(1024)S(1)} %rsqrt.44) | copy-start | bytes 9412
  19.4 83.2 %copy-start.5 = (bf16[2,1,7,112,256]{4,3,2,1,0:T(8,128)(2,1)S(1)}, bf16[2,1,7,112,256]{4,3,2,1,0:T(8,128)(2,1)}, u32[]{:S(2)}) copy-start(bf16[2,1,7,112,256]{4,3,2,1,0:T(8,128)(2,1)} %param.34) | copy-start | bytes 2408452
  107.2 47.5 %all-to-all-start = ((bf16[1,7,112,384]{3,1,0,2:T(8,128)(2,1)}), bf16[1,7,112,384]{3,1,0,2:T(8,128)(2,1)}, u32[]{:S(2)}, u32[]{:S(2)}) async-start(bf16[1,7,112,384]{3,1,0,2:T(8,128)(2,1)} %pad_maximum_fusion.4), calls=%async_computation | async-start | bytes 1376256 | tf_op jit(solution)/shard_map/all_to_all | solution.py:230
  112.9 20.0 %copy-start.41 = (bf16[784,128]{0,1:T(8,128)(2,1)}, bf16[784,128]{0,1:T(8,128)(2,1)S(1)}, u32[]{:S(2)}) copy-start(bf16[784,128]{0,1:T(8,128)(2,1)S(1)} %copy.518) | copy-start | bytes 602116
  113.1 19.8 %copy-start.52 = (bf16[784,128]{0,1:T(8,128)(2,1)}, bf16[784,128]{0,1:T(8,128)(2,1)S(1)}, u32[]{:S(2)}) copy-start(bf16[784,128]{0,1:T(8,128)(2,1)S(1)} %copy.517) | copy-start | bytes 602116
  142.6 18.3 %copy-start.34 = (bf16[2,1,7,112,256]{4,3,2,1,0:T(8,128)(2,1)S(1)}, bf16[2,1,7,112,256]{4,3,2,1,0:T(8,128)(2,1)}, u32[]{:S(2)}) copy-start(bf16[2,1,7,112,256]{4,3,2,1,0:T(8,128)(2,1)} %param.35) | copy-start | bytes 2408452
  143.3 18.3 %copy-start.136 = (f32[4,784]{1,0:T(4,128)S(1)}, f32[4,784]{1,0:T(4,128)}, u32[]{:S(2)}) copy-start(f32[4,784]{1,0:T(4,128)} %copy-done.135) | copy-start | bytes 37636
  148.3 14.3 %copy-start.138 = (f32[7,112]{1,0:T(8,128)S(1)}, f32[7,112]{1,0:T(8,128)}, u32[]{:S(2)}) copy-start(f32[7,112]{1,0:T(8,128)} %copy-done.137) | copy-start | bytes 9412
  148.3 14.3 %copy-start.140 = (f32[7,112]{1,0:T(8,128)S(1)}, f32[7,112]{1,0:T(8,128)}, u32[]{:S(2)}) copy-start(f32[7,112]{1,0:T(8,128)} %copy-done.139) | copy-start | bytes 9412
  154.8 23.2 %all-to-all-start.2 = ((bf16[1,7,112,384]{3,1,0,2:T(8,128)(2,1)}), bf16[1,7,112,384]{3,1,0,2:T(8,128)(2,1)S(1)}, u32[]{:S(2)}, u32[]{:S(2)}) async-start(bf16[1,7,112,384]{3,1,0,2:T(8,128)(2,1)} %pad_maximum_fusion.5), calls=%async_computation.2 | async-start | bytes 1376256 | tf_op jit(solution)/shard_map/all_to_all | solution.py:230
  179.7 17.8 %copy-start.39 = (bf16[784,128]{0,1:T(8,128)(2,1)}, bf16[784,128]{0,1:T(8,128)(2,1)S(1)}, u32[]{:S(2)}) copy-start(bf16[784,128]{0,1:T(8,128)(2,1)S(1)} %copy.360) | copy-start | bytes 602116
  182.4 28.7 %copy-start.29 = (f32[1,112,7,128]{3,1,2,0:T(8,128)}, f32[1,112,7,128]{3,1,2,0:T(8,128)S(1)}, u32[]{:S(2)}) copy-start(f32[1,112,7,128]{3,1,2,0:T(8,128)S(1)} %copy.364) | copy-start | bytes 1204228
  209.6 25.7 %copy-start.153 = (f32[1,256]{1,0:T(1,128)S(1)}, f32[1,256]{1,0:T(1,128)}, u32[]{:S(2)}) copy-start(f32[1,256]{1,0:T(1,128)} %get-tuple-element.444) | copy-start | bytes 3076
  215.5 14.5 %all-to-all-start.1 = ((bf16[1,112,7,128]{3,2,0,1:T(8,128)(2,1)}), bf16[1,112,7,128]{3,2,0,1:T(8,128)(2,1)S(1)}, u32[]{:S(2)}, u32[]{:S(2)}) async-start(bf16[1,112,7,128]{3,2,0,1:T(8,128)(2,1)} %copy.367), calls=%async_computation.1 | async-start | bytes 458752 | tf_op jit(solution)/shard_map/all_to_all | solution.py:245
  221.2 26.2 %copy-start.35 = (f32[1,1,7,112,256]{4,3,2,1,0:T(8,128)S(1)}, f32[1,1,7,112,256]{4,3,2,1,0:T(8,128)}, u32[]{:S(2)}) copy-start(f32[1,1,7,112,256]{4,3,2,1,0:T(8,128)} %get-tuple-element.387) | copy-start | bytes 2408452
  229.9 13.9 %all-to-all-start.3 = ((bf16[1,112,7,128]{3,2,0,1:T(8,128)(2,1)}), bf16[1,112,7,128]{3,2,0,1:T(8,128)(2,1)}, u32[]{:S(2)}, u32[]{:S(2)}) async-start(bf16[1,112,7,128]{3,2,0,1:T(8,128)(2,1)} %copy.391), calls=%async_computation.3 | async-start | bytes 458752 | tf_op jit(solution)/shard_map/all_to_all | solution.py:245
  235.3 13.9 %copy-start.49 = (bf16[256,1024]{1,0:T(8,128)(2,1)S(1)}, bf16[256,1024]{1,0:T(8,128)(2,1)}, u32[]{:S(2)}) copy-start(bf16[256,1024]{1,0:T(8,128)(2,1)} %get-tuple-element.342) | copy-start | bytes 1572868
  235.3 13.9 %copy-start.149 = (f32[1,256]{1,0:T(1,128)S(1)}, f32[1,256]{1,0:T(1,128)}, u32[]{:S(2)}) copy-start(f32[1,256]{1,0:T(1,128)} %get-tuple-element.443) | copy-start | bytes 3076
  235.3 13.9 %copy-start.157 = (f32[1,256]{1,0:T(1,128)S(1)}, f32[1,256]{1,0:T(1,128)}, u32[]{:S(2)}) copy-start(f32[1,256]{1,0:T(1,128)} %get-tuple-element.442) | copy-start | bytes 3076
  237.1 36.7 %copy-start.16 = (f32[784,256]{1,0:T(8,128)}, f32[784,256]{1,0:T(8,128)S(1)}, u32[]{:S(2)}) copy-start(f32[784,256]{1,0:T(8,128)S(1)} %get-tuple-element.495) | copy-start | bytes 2408452
  248.8 25.1 %copy-start.7 = (f32[784,256]{1,0:T(8,128)}, f32[784,256]{1,0:T(8,128)S(1)}, u32[]{:S(2)}) copy-start(f32[784,256]{1,0:T(8,128)S(1)} %get-tuple-element.497) | copy-start | bytes 2408452
  248.8 25.0 %copy-start.128 = (f32[784]{0:T(1024)}, f32[784]{0:T(1024)S(1)}, u32[]{:S(2)}) copy-start(f32[784]{0:T(1024)S(1)} %broadcast_multiply_fusion.27) | copy-start | bytes 9412
  249.2 24.7 %copy-start.130 = (f32[784]{0:T(1024)}, f32[784]{0:T(1024)S(1)}, u32[]{:S(2)}) copy-start(f32[784]{0:T(1024)S(1)} %add_rsqrt_fusion) | copy-start | bytes 9412
  249.9 16.0 %copy-start.74 = (bf16[1,1,7,112,256]{4,3,2,1,0:T(8,128)(2,1)S(1)}, bf16[1,1,7,112,256]{4,3,2,1,0:T(8,128)(2,1)}, u32[]{:S(2)}) copy-start(bf16[1,1,7,112,256]{4,3,2,1,0:T(8,128)(2,1)} %get-tuple-element.382) | copy-start | bytes 1204228
  249.9 16.0 %copy-start.233 = (bf16[1024,256]{1,0:T(8,128)(2,1)S(1)}, bf16[1024,256]{1,0:T(8,128)(2,1)}, u32[]{:S(2)}) copy-start(bf16[1024,256]{1,0:T(8,128)(2,1)} %get-tuple-element.343) | copy-start | bytes 1572868
  286.5 22.7 %slice-start.6 = ((s8[11239424]{0:T(1024)(128)(4,1)}), s8[2850816]{0:T(1024)(128)(4,1)S(1)}, s32[]{:S(2)}) async-start(s8[11239424]{0:T(1024)(128)(4,1)} %bitcast.521), calls=%async_computation.15 | async-start | bytes 5701632
  294.9 14.3 %slice-start.7 = ((s8[11239424]{0:T(1024)(128)(4,1)}), s8[4194304]{0:T(1024)(128)(4,1)S(1)}, s32[]{:S(2)}) async-start(s8[11239424]{0:T(1024)(128)(4,1)} %bitcast.521), calls=%async_computation.16 | async-start | bytes 8388608
  344.4 39.8 %all-to-all-start.6 = ((bf16[1,7,112,128]{3,1,0,2:T(8,128)(2,1)}), bf16[1,7,112,128]{3,1,0,2:T(8,128)(2,1)S(1)}, u32[]{:S(2)}, u32[]{:S(2)}) async-start(bf16[1,7,112,128]{3,1,0,2:T(8,128)(2,1)} %copy.531), calls=%async_computation.6 | async-start | bytes 458752 | tf_op jit(solution)/shard_map/all_to_all | solution.py:296
  384.3 27.3 %all-to-all-start.4 = ((bf16[1,7,112,128]{3,1,0,2:T(8,128)(2,1)}), bf16[1,7,112,128]{3,1,0,2:T(8,128)(2,1)S(1)}, u32[]{:S(2)}, u32[]{:S(2)}) async-start(bf16[1,7,112,128]{3,1,0,2:T(8,128)(2,1)} %copy.529), calls=%async_computation.4 | async-start | bytes 458752 | tf_op jit(solution)/shard_map/all_to_all | solution.py:296
  442.8 41.7 %all-to-all-start.7 = ((bf16[1,112,7,384]{3,2,0,1:T(8,128)(2,1)}), bf16[1,112,7,384]{3,2,0,1:T(8,128)(2,1)}, u32[]{:S(2)}, u32[]{:S(2)}) async-start(bf16[1,112,7,384]{3,2,0,1:T(8,128)(2,1)} %maximum_bitcast_fusion.3), calls=%async_computation.7 | async-start | bytes 1376256 | tf_op jit(solution)/shard_map/all_to_all | solution.py:308
  474.0 17.2 %copy-start.227 = (f32[128]{0:T(128)S(1)}, f32[128]{0:T(128)}, u32[]{:S(2)}) copy-start(f32[128]{0:T(128)} %get-tuple-element.339) | copy-start | bytes 1540
  474.0 17.9 %copy-start.228 = (f32[128]{0:T(128)S(1)}, f32[128]{0:T(128)}, u32[]{:S(2)}) copy-start(f32[128]{0:T(128)} %get-tuple-element.338) | copy-start | bytes 1540
  484.5 23.3 %all-to-all-start.5 = ((bf16[1,112,7,384]{3,2,0,1:T(8,128)(2,1)}), bf16[1,112,7,384]{3,2,0,1:T(8,128)(2,1)}, u32[]{:S(2)}, u32[]{:S(2)}) async-start(bf16[1,112,7,384]{3,2,0,1:T(8,128)(2,1)} %maximum_bitcast_fusion.2), calls=%async_computation.5 | async-start | bytes 1376256 | tf_op jit(solution)/shard_map/all_to_all | solution.py:308
  490.6 219.8 %all-reduce.81.cloned.1.call-start = ((), (), s32[]{:S(2)}) async-start(), calls=%async_computation.8 | async-start | bytes 6291456 | tf_op jit(solution)/shard_map/psum | solution.py:348
  495.8 14.6 %copy-start.19 = (bf16[1,7,112,768]{3,2,1,0:T(8,128)(2,1)S(1)}, bf16[1,7,112,768]{3,2,1,0:T(8,128)(2,1)}, u32[]{:S(2)}) copy-start(bf16[1,7,112,768]{3,2,1,0:T(8,128)(2,1)} %slice_dynamic-update-slice_fusion.4) | copy-start | bytes 3612676
  496.3 15.3 %copy-start.82 = (bf16[1,784,256]{2,1,0:T(8,128)(2,1)S(1)}, bf16[1,784,256]{2,1,0:T(8,128)(2,1)}, u32[]{:S(2)}) copy-start(bf16[1,784,256]{2,1,0:T(8,128)(2,1)} %copy-done.81) | copy-start | bytes 1204228
  528.3 43.5 %copy-start.12 = (f32[784,256]{1,0:T(8,128)S(1)}, f32[784,256]{1,0:T(8,128)}, u32[]{:S(2)}) copy-start(f32[784,256]{1,0:T(8,128)} %copy-done.11) | copy-start | bytes 2408452
  528.3 43.5 %copy-start.156 = (f32[1,256]{1,0:T(1,128)S(1)}, f32[1,256]{1,0:T(1,128)}, u32[]{:S(2)}) copy-start(f32[1,256]{1,0:T(1,128)} %copy-done.154) | copy-start | bytes 3076
  571.8 138.6 %copy-start.96 = (f32[256,256]{1,0:T(8,128)S(1)}, f32[256,256]{1,0:T(8,128)}, u32[]{:S(2)}) copy-start(f32[256,256]{1,0:T(8,128)} %param.52) | copy-start | bytes 786436
  574.9 135.6 %copy-start.15 = (f32[768,768]{1,0:T(8,128)S(1)}, f32[768,768]{1,0:T(8,128)}, u32[]{:S(2)}) copy-start(f32[768,768]{1,0:T(8,128)} %param.50) | copy-start | bytes 7077892
  712.0 21.0 %copy-start.23 = (f32[1,256,1024]{2,1,0:T(8,128)S(1)}, f32[1,256,1024]{2,1,0:T(8,128)}, u32[]{:S(2)}) copy-start(f32[1,256,1024]{2,1,0:T(8,128)} %param.39) | copy-start | bytes 3145732
  712.0 21.0 %copy-start.25 = (f32[256,1024]{1,0:T(8,128)S(1)}, f32[256,1024]{1,0:T(8,128)}, u32[]{:S(2)}) copy-start(f32[256,1024]{1,0:T(8,128)} %get-tuple-element.550) | copy-start | bytes 3145732
  (195 other events, 903.3 us)
Sparse Core Ops, SparseCore 0:
  571.9 138.5 all-reduce.80
where the time goes:
time: 754 us; the launch traced here: 746 us
  waiting for transfers between devices  169 us (22%)
  matrix products  156 us (21%)
  local copies, waits for them, and re-layouts  121 us (16%)
  blocking collectives  121 us (16%)
  other arithmetic  115 us (15%)
  starting transfers between devices  42.5 us (6%)
  between operations  20.4 us (3%)
    psum x1, waiting for transfers between devices, per_device(): lax.psum((totals[0], totals[1], totals[2], totals[3], totals[4]), ('band'...  135 us
    psum x1, blocking collectives, per_device(): lax.psum((own_slot(weight_qkv, owners[0], device_index), own_slot(weight_...  80.7 us
    unnamed x492, local copies, waits for them, and re-layouts  40.7 us
    psum x1, blocking collectives, per_device(): lax.psum((totals[0], totals[1], totals[2], totals[3], totals[4]), ('band'...  40.2 us
    dot_general x4, matrix products, attend_backward(): jnp.einsum('hqk,qhd->khd', softmax_f.astype(jnp.bfloat16), grad_h, prefer...  23.3 us
    dot_general x4, matrix products, attend_backward(): jnp.einsum('qhd,khd->hqk', grad_h, value_h, preferred_element_type=jnp.fl...  22.4 us
    convert_element_type x4, other arithmetic, attend_backward(): grad_scores = (softmax_f * (grad_soft - inner_sum)).astype(jnp.bfloat16)  20.7 us
    reduce_sum x6, other arithmetic, position_conv(): padded[:, row_off:row_off + rows_n, col_off:col_off + cols_n, :]  18.6 us
  transfers between devices with their start and end apart: 9, of which 5 were waited for; matrix products, arithmetic and copies ran while one was open for 20% of the time, Pallas kernels for 0%

commit v1 on v0

v1 whole, which is shorter than its diff:
```python
import functools

import jax
import jax.numpy as jnp
from jax import lax
from jax.experimental import pallas as pl
from jax.experimental.pallas import tpu as pltpu
from jax.sharding import PartitionSpec as P

HEAD_DIM = 32
STRIPE = 7
STEP = 10
EPS_NORM = 1e-05
BETA_ONE = 0.5
BETA_TWO = 0.6
RATE = 0.04
RATE_VECTORS = 0.2
DECAY = 0.01
EPS_ADAM = 1e-08
MESH = pl.DeviceIdType.MESH
F32 = jnp.float32
BF16 = jnp.bfloat16
PIECE = 64
LOG2E = 1.4426950408889634
LN2 = 0.6931471805599453
Q_SCALE = LOG2E * HEAD_DIM**-0.5
VMEM_LIMIT = 60 * 1024 * 1024
ROW_QKV, ROW_PROJ, ROW_FC1, ROW_FC2, ROW_END = 0, 768, 1024, 2048, 3072


def mm(a, b):
    return lax.dot_general(a, b, (((1,), (0,)), ((), ())), preferred_element_type=F32)


def mm_nt(a, b):
    return lax.dot_general(a, b, (((1,), (1,)), ((), ())), preferred_element_type=F32)


def mm_tn(a, b):
    return lax.dot_general(a, b, (((0,), (0,)), ((), ())), preferred_element_type=F32)


def exchange_kernel(n, piece, x_ref, o_ref, send_sem, recv_sem, loc_sem):
    me = lax.axis_index("band")
    bar = pltpu.get_barrier_semaphore()

    def greet(k, c):
        pl.semaphore_signal(
            bar, inc=1, device_id={"band": lax.rem(me + k, n)}, device_id_type=MESH
        )
        return c

    lax.fori_loop(1, n, greet, 0)
    pl.semaphore_wait(bar, n - 1)

    def rows(i):
        return pl.ds(pl.multiple_of(i * piece, piece), piece)

    def send(k, c):
        d = lax.rem(me + k, n)
        pltpu.make_async_remote_copy(
            src_ref=x_ref.at[rows(d)],
            dst_ref=o_ref.at[rows(me)],
            send_sem=send_sem.at[k],
            recv_sem=recv_sem.at[k],
            device_id={"band": d},
            device_id_type=MESH,
        ).start()
        return c

    lax.fori_loop(1, n, send, 0)
    local = pltpu.make_async_copy(x_ref.at[rows(me)], o_ref.at[rows(me)], loc_sem)
    local.start()
    local.wait()

    def take(k, c):
        s = lax.rem(me - k + n, n)
        pltpu.make_async_remote_copy(
            src_ref=x_ref.at[rows(s)],
            dst_ref=o_ref.at[rows(s)],
            send_sem=send_sem.at[k],
            recv_sem=recv_sem.at[k],
            device_id={"band": s},
            device_id_type=MESH,
        ).wait()
        return c

    lax.fori_loop(1, n, take, 0)


def exchange(x, n, cid):
    return pl.pallas_call(
        functools.partial(exchange_kernel, n, x.shape[0] // n),
        out_shape=jax.ShapeDtypeStruct(x.shape, x.dtype),
        in_specs=[pl.BlockSpec(memory_space=pltpu.VMEM)],
        out_specs=pl.BlockSpec(memory_space=pltpu.VMEM),
        scratch_shapes=[
            pltpu.SemaphoreType.DMA((n,)),
            pltpu.SemaphoreType.DMA((n,)),
            pltpu.SemaphoreType.DMA,
        ],
        compiler_params=pltpu.CompilerParams(
            collective_id=cid, has_side_effects=True, vmem_limit_bytes=VMEM_LIMIT
        ),
        name="exchange",
    )(x)


def sum_kernel(nb, nx, total_rows, x_ref, o_ref, got, half, recv, s1, r1, s2, r2, s3, r3, s4, r4):
    nq = (nb // 2) * nx
    p = total_rows // (2 * nq)
    band = lax.axis_index("band")
    core = lax.rem(band, 2)
    q = (band // 2) * nx + lax.axis_index("batch")
    sibling = {"band": band + 1 - 2 * core}
    bar = pltpu.get_barrier_semaphore()

    def chip(t):
        return {"band": (t // nx) * 2 + core, "batch": lax.rem(t, nx)}

    def ahead(k):
        return lax.rem(q + k, nq)

    def behind(k):
        return lax.rem(q - k + nq, nq)

    def copy(src, dst, ss, rs, dev):
        return pltpu.make_async_remote_copy(
            src_ref=src, dst_ref=dst, send_sem=ss, recv_sem=rs, device_id=dev, device_id_type=MESH
        )

    def loop(lo, hi, body):
        def step(k, c):
            body(k)
            return c

        lax.fori_loop(lo, hi, step, 0)

    pl.semaphore_signal(bar, inc=1, device_id=sibling, device_id_type=MESH)
    loop(
        1,
        nq,
        lambda k: pl.semaphore_signal(
            bar, inc=1, device_id=chip(ahead(k)), device_id_type=MESH
        ),
    )
    pl.semaphore_wait(bar, nq)

    def whole_rows(c, t):
        return pl.ds(pl.multiple_of((c * nq + t) * p, 16), p)

    def half_rows(t):
        return pl.ds(pl.multiple_of(t * p, 16), p)

    def pair_copy(k, side):
        t = ahead(k)
        return copy(
            x_ref.at[whole_rows(side, t)], got.at[half_rows(t)], s1.at[t], r1.at[t], sibling
        )

    loop(1, nq + 1, lambda k: pair_copy(k, 1 - core).start())

    def scatter_copy(k):
        t = ahead(k)
        return copy(half.at[half_rows(t)], recv.at[half_rows(q)], s2.at[k], r2.at[k], chip(t))

    def pair_sum(k):
        t = ahead(k)
        pair_copy(k, core).wait()
        half[half_rows(t)] = (
            x_ref[whole_rows(core, t)].astype(F32) + got[half_rows(t)].astype(F32)
        ).astype(BF16)

        @pl.when(k < nq)
        def _():
            scatter_copy(k).start()

    loop(1, nq + 1, pair_sum)

    def add_piece(k, acc):
        t = behind(k)
        copy(half.at[half_rows(t)], recv.at[half_rows(t)], s2.at[k], r2.at[k], chip(t)).wait()
        return acc + recv[half_rows(t)].astype(F32)

    total = lax.fori_loop(1, nq, add_piece, half[half_rows(q)].astype(F32))
    mine = o_ref.at[whole_rows(core, q)]
    o_ref[whole_rows(core, q)] = total.astype(BF16)

    def gather_copy(k):
        return copy(mine, mine, s3.at[k], r3.at[k], chip(ahead(k)))

    def pass_on(t, side):
        return copy(
            o_ref.at[whole_rows(core, t)],
            o_ref.at[whole_rows(side, t)],
            s4.at[t],
            r4.at[t],
            sibling,
        )

    loop(1, nq, lambda k: gather_copy(k).start())
    pass_on(q, core).start()

    def relay(k):
        t = behind(k)
        copy(mine, o_ref.at[whole_rows(core, t)], s3.at[k], r3.at[k], chip(t)).wait()
        pass_on(t, core).start()

    loop(1, nq, relay)
    loop(0, nq, lambda t: pass_on(t, 1 - core).wait())


def sum_everywhere(x, nb, nx, cid):
    rows, cols = x.shape
    nq = nb // 2 * nx
    unit = 32 * nq
    padded = -(-rows // unit) * unit
    if padded != rows:
        x = jnp.concatenate([x, jnp.zeros((padded - rows, cols), x.dtype)], axis=0)
    sems = [pltpu.SemaphoreType.DMA((nq,)) for _ in range(8)]
    out = pl.pallas_call(
        functools.partial(sum_kernel, nb, nx, padded),
        out_shape=jax.ShapeDtypeStruct(x.shape, x.dtype),
        in_specs=[pl.BlockSpec(memory_space=pltpu.VMEM)],
        out_specs=pl.BlockSpec(memory_space=pltpu.VMEM),
        scratch_shapes=[pltpu.VMEM((padded // 2, cols), x.dtype)] * 3 + sems,
        compiler_params=pltpu.CompilerParams(
            collective_id=cid, has_side_effects=True, vmem_limit_bytes=VMEM_LIMIT
        ),
        name="sum_everywhere",
    )(x)
    return out


def order_out(pieces_n, length):
    row = lax.broadcasted_iota(jnp.int32, (pieces_n * PIECE, 1), 0)
    s = row // PIECE
    m = row % PIECE
    a = (m * 37) // 256
    b = m - STRIPE * a
    token = jnp.where(m < STRIPE * STRIPE, a * length + STRIPE * s + b, -1)
    column = lax.broadcasted_iota(jnp.int32, (pieces_n * PIECE, STRIPE * length), 1)
    return jnp.where(column == token, 1.0, 0.0).astype(BF16)


def order_in(pieces_n, length):
    row = lax.broadcasted_iota(jnp.int32, (1, pieces_n * PIECE), 1)
    s = row // PIECE
    m = row % PIECE
    a = (m * 37) // 256
    b = m - STRIPE * a
    token = jnp.where(m < STRIPE * STRIPE, b * length + STRIPE * s + a, -1)
    column = lax.broadcasted_iota(jnp.int32, (STRIPE * length, pieces_n * PIECE), 0)
    return jnp.where(column == token, 1.0, 0.0).astype(BF16)


def unit_rows(values):
    centred = values - jnp.mean(values, axis=-1, keepdims=True)
    inverse = lax.rsqrt(jnp.mean(centred * centred, axis=-1, keepdims=True) + EPS_NORM)
    return centred * inverse, inverse


def norm_back(grad_normed, gain, unit, inverse):
    scaled = grad_normed * gain
    first_mean = jnp.mean(scaled, axis=-1, keepdims=True)
    second_mean = jnp.mean(scaled * unit, axis=-1, keepdims=True)
    return inverse * (scaled - first_mean - unit * second_mean)


def shifted_columns(v, length):
    tokens = v.shape[0]
    column = lax.broadcasted_iota(jnp.int32, v.shape, 0) % length
    before = jnp.where(column == 0, 0.0, pltpu.roll(v, 1, 0))
    after = jnp.where(column == length - 1, 0.0, pltpu.roll(v, tokens - 1, 0))
    return before, v, after


def shifted_rows(v, length):
    zeros = jnp.zeros((length, v.shape[1]), v.dtype)
    above = jnp.concatenate([zeros, v[: v.shape[0] - length]], axis=0)
    below = jnp.concatenate([v[length:], zeros], axis=0)
    return above, v, below


def tap_row(half, a, b):
    return 12 + (3 * a + b if half == 0 else 3 * b + a)


def conv(v, vec_ref, lanes, half, length, flipped):
    total = jnp.zeros_like(v)
    for b, col in enumerate(shifted_columns(v, length)):
        for a, val in enumerate(shifted_rows(col, length)):
            row = tap_row(half, 2 - a, 2 - b) if flipped else tap_row(half, a, b)
            total = total + val * vec_ref[row : row + 1, lanes]
    return total


def head_mask(shape, h, offset=0):
    lane = lax.broadcasted_iota(jnp.int32, shape, len(shape) - 1) - offset
    return (lane >= h * HEAD_DIM) & (lane < (h + 1) * HEAD_DIM)


def three_parts(x):
    lane = lax.broadcasted_iota(jnp.int32, x.shape, len(x.shape) - 1) % HEAD_DIM
    hi = x.astype(BF16).astype(F32)
    mid = (x - hi).astype(BF16).astype(F32)
    low = x - hi - mid
    parts = jnp.where(lane == 0, hi, jnp.where(lane == 1, mid, jnp.where(lane == 2, low, 0.0)))
    return parts.astype(BF16)


def stack_heads(block, with_ones):
    lane = lax.broadcasted_iota(jnp.int32, block.shape, 1)
    rows = []
    for h in range(4):
        keep = head_mask(block.shape, h)
        part = jnp.where(keep, block, 0.0)
        if with_ones:
            ones = jnp.where(keep & (lane % HEAD_DIM < 3), 1.0, 0.0)
            part = jnp.concatenate([part, ones], axis=1)
        rows.append(part.astype(BF16))
    return jnp.concatenate(rows, axis=0)


def pick_heads(stacked, r):
    out = stacked[:r]
    for h in range(1, 4):
        out = jnp.where(head_mask(out.shape, h), stacked[h * r : (h + 1) * r], out)
    return out


def lane_blocks(w_ref, half):
    return lambda b: w_ref[256 * b : 256 * b + 256, 128 * half : 128 * half + 128]


def attention_forward(x, half, length, wb, vec_ref, qa_ref, k_ref, v_ref, o_ref, att_ref, vx_ref):
    tokens = x.shape[0]
    lanes = slice(128 * half, 128 * half + 128)
    unit, _ = unit_rows(x)
    normed = (unit * vec_ref[0:1] + vec_ref[1:2]).astype(BF16)
    q = (mm(normed, wb(0)) + vec_ref[2:3, lanes]) * Q_SCALE
    k = mm(normed, wb(1))
    v = mm(normed, wb(2)) + vec_ref[3:4, lanes]
    qa_ref[:, 0:128] = q.astype(BF16)
    k_ref[...] = k.astype(BF16)
    v_ref[...] = v.astype(BF16)
    vx_ref[:, 0:128] = v.astype(BF16)
    vx_ref[:, 128:256] = jnp.ones((tokens, 128), BF16)
    r = 112

    def block(i, c):
        rows = pl.ds(pl.multiple_of(i * r, r), r)
        qs = stack_heads(qa_ref[rows, 0:128].astype(F32), False)
        scores = mm_nt(qs, k_ref[...])
        highest = jnp.max(scores, axis=-1, keepdims=True)
        probs = jnp.exp2(scores - highest).astype(BF16)
        both = mm(probs, vx_ref[...])
        weighted = pick_heads(both[:, 0:128], r)
        total = pick_heads(both[:, 128:256], r)
        top = pick_heads(jnp.broadcast_to(highest, (4 * r, 128)), r)
        o_ref[rows, :] = weighted / total
        qa_ref[rows, 128:256] = three_parts(-(top + jnp.log2(total)))
        return c

    lax.fori_loop(0, tokens // r, block, 0)
    lepe = conv(v_ref[...].astype(F32), vec_ref, lanes, half, length, False)
    att_ref[...] = (o_ref[...] + lepe + vec_ref[21:22, lanes]).astype(BF16)


def attention_backward(
    x, half, length, grad, wb, vec_ref, qa_ref, k_ref, v_ref, o_ref, da_ref, dq_ref, dk_ref, dv_ref, gw_ref, rows_ref
):
    tokens = x.shape[0]
    lanes = slice(128 * half, 128 * half + 128)
    grad_f = grad.astype(F32)
    product = grad_f * o_ref[...]
    inner = jnp.zeros_like(product)
    for h in range(4):
        keep = head_mask(product.shape, h)
        inner = jnp.where(
            keep, jnp.sum(jnp.where(keep, product, 0.0), axis=-1, keepdims=True), inner
        )
    da_ref[:, 0:128] = grad
    da_ref[:, 128:256] = three_parts(-inner)
    dq_ref[...] = jnp.zeros_like(dq_ref)
    r = 112

    def block(i, c):
        rows = pl.ds(pl.multiple_of(i * r, r), r)
        kb = k_ref[rows, :].astype(F32)
        ks = stack_heads(kb, True)
        vs = stack_heads(v_ref[rows, :].astype(F32), True)
        p = jnp.exp2(mm_nt(ks, qa_ref[...]))
        ds = (p * mm_nt(vs, da_ref[...])).astype(BF16)
        dv_ref[rows, :] = pick_heads(mm(p.astype(BF16), da_ref[:, 0:128]), r)
        dk_ref[rows, :] = pick_heads(mm(ds, qa_ref[:, 0:128]), r)
        dq_ref[...] += mm_tn(ks[:, 0:128], ds)
        return c

    lax.fori_loop(0, tokens // r, block, 0)
    dq = (jnp.transpose(dq_ref[...]) * HEAD_DIM**-0.5).astype(BF16)
    dk = (dk_ref[...] * LN2).astype(BF16)
    dv = (dv_ref[...] + conv(grad_f, vec_ref, lanes, half, length, True)).astype(BF16)
    unit, _ = unit_rows(x)
    normed = (unit * vec_ref[0:1] + vec_ref[1:2]).astype(BF16)
    gw_ref[...] += mm_tn(normed, jnp.concatenate([dq, dk, dv], axis=1))
    rows_ref[0:1, :] += jnp.sum(dq.astype(F32), axis=0, keepdims=True)
    rows_ref[1:2, :] += jnp.sum(dv.astype(F32), axis=0, keepdims=True)
    for b, col in enumerate(shifted_columns(v_ref[...].astype(F32), length)):
        for a, val in enumerate(shifted_rows(col, length)):
            row = tap_row(half, a, b) - 10
            rows_ref[row : row + 1, :] += jnp.sum(grad_f * val, axis=0, keepdims=True)
    rows_ref[11:12, :] += jnp.sum(grad_f, axis=0, keepdims=True)
    part = mm_nt(dq, wb(0)) + mm_nt(dk, wb(1)) + mm_nt(dv, wb(2))
    gain_row = jnp.sum(part * unit, axis=0, keepdims=True)
    shift_row = jnp.sum(part, axis=0, keepdims=True)
    for i in range(2):
        rows_ref[12 + i : 13 + i, :] += gain_row[:, 128 * i : 128 * i + 128]
        rows_ref[14 + i : 15 + i, :] += shift_row[:, 128 * i : 128 * i + 128]
    return part


def feed_forward(x, att, top, w_ref, base, vec_ref, n2_ref, acc_ref, gn_ref, gp_ref, g1_ref, g2_ref, rows_ref):
    middle = x + mm(att, w_ref[base : base + 256, :]) + vec_ref[4:5]
    unit, inverse = unit_rows(middle)
    n2_ref[...] = (unit * vec_ref[5:6] + vec_ref[6:7]).astype(BF16)
    acc_ref[...] = middle + vec_ref[11:12]
    gn_ref[...] = jnp.zeros_like(gn_ref)
    for f in range(4):
        w1 = w_ref[base + 256 * (1 + f) : base + 256 * (2 + f), :]
        w2 = w_ref[base + 256 * (5 + f) : base + 256 * (6 + f), :]
        cols = slice(256 * f, 256 * f + 256)
        hidden = mm(n2_ref[...], w1) + vec_ref[7 + f : 8 + f]
        below = 0.5 * (1.0 + lax.erf(hidden * (0.5**0.5)))
        active = (hidden * below).astype(BF16)
        slope = below + hidden * jnp.exp(-0.5 * hidden * hidden) * 0.3989422804014327
        grad_hidden = (mm_nt(top, w2) * slope).astype(BF16)
        acc_ref[...] += mm(active, w2)
        gn_ref[...] += mm_nt(grad_hidden, w1)
        g1_ref[:, cols] += mm_tn(n2_ref[...], grad_hidden)
        g2_ref[:, cols] += mm_tn(top, active)
        rows_ref[3 + f : 4 + f, :] += jnp.sum(grad_hidden.astype(F32), axis=0, keepdims=True)
    grad_normed = gn_ref[...]
    top_f = top.astype(F32)
    grad_middle = top_f + norm_back(grad_normed, vec_ref[5:6], unit, inverse)
    branch = grad_middle.astype(BF16)
    gp_ref[...] += mm_tn(branch, att)
    rows_ref[0:1, :] += jnp.sum(branch.astype(F32), axis=0, keepdims=True)
    rows_ref[1:2, :] += jnp.sum(grad_normed * unit, axis=0, keepdims=True)
    rows_ref[2:3, :] += jnp.sum(grad_normed, axis=0, keepdims=True)
    rows_ref[7:8, :] += jnp.sum(top_f, axis=0, keepdims=True)
    grad_att = mm_nt(branch, w_ref[base : base + 256, :]).astype(BF16)
    return acc_ref[...].astype(BF16), grad_middle, grad_att


PARAMS = pltpu.CompilerParams(
    dimension_semantics=("arbitrary",), vmem_limit_bytes=VMEM_LIMIT
)


def whole(shape):
    return pl.BlockSpec(shape, lambda m: (0,) * len(shape))


def each(shape):
    return pl.BlockSpec((None,) + shape, lambda m: (m,) + (0,) * len(shape))


def shape_of(dtype, *shape):
    return jax.ShapeDtypeStruct(shape, dtype)


def pack_tokens(x, nb, length):
    micro, tokens, channels = x.shape

    def kernel(x_ref, o_ref, hot):
        @pl.when(pl.program_id(0) == 0)
        def _():
            hot[...] = order_out(nb, length)

        o_ref[...] = mm(hot[...], x_ref[...]).astype(BF16)

    return pl.pallas_call(
        kernel,
        grid=(micro,),
        in_specs=[each((tokens, channels))],
        out_specs=each((nb * PIECE, channels)),
        out_shape=shape_of(BF16, micro, nb * PIECE, channels),
        scratch_shapes=[pltpu.VMEM((nb * PIECE, tokens), BF16)],
        compiler_params=PARAMS,
        name="pack_tokens",
    )(x)


def forward_call(x, half, nb, length, weights, vectors):
    micro = x.shape[0]
    tokens = STRIPE * length
    packed = nb * PIECE

    def kernel(x_ref, w_ref, vec_ref, qa_ref, k_ref, v_ref, o_ref, att_ref, xs_ref, vx_ref, *scr):
        if half == 0:
            attention_forward(
                x_ref[...].astype(F32), half, length, lane_blocks(w_ref, half), vec_ref, qa_ref, k_ref, v_ref, o_ref, att_ref, vx_ref
            )
        else:
            att_s, hot_in, hot_out = scr

            @pl.when(pl.program_id(0) == 0)
            def _():
                hot_in[...] = order_in(nb, length)
                hot_out[...] = order_out(nb, length)

            xs_ref[...] = mm(hot_in[...], x_ref[...]).astype(BF16)
            attention_forward(
                xs_ref[...].astype(F32), half, length, lane_blocks(w_ref, half), vec_ref, qa_ref, k_ref, v_ref, o_ref, att_s, vx_ref
            )
            att_ref[...] = mm(hot_out[...], att_s[...]).astype(BF16)

    rows = tokens if half == 0 else packed
    scratch = [pltpu.VMEM((tokens, 256), BF16)]
    if half == 1:
        scratch += [
            pltpu.VMEM((tokens, 128), BF16),
            pltpu.VMEM((tokens, packed), BF16),
            pltpu.VMEM((packed, tokens), BF16),
        ]
    if half == 0:
        def body(x_ref, w_ref, vec_ref, qa_ref, k_ref, v_ref, o_ref, att_ref, *scr):
            kernel(x_ref, w_ref, vec_ref, qa_ref, k_ref, v_ref, o_ref, att_ref, None, *scr)
        extra_specs, extra_shapes = [], []
    else:
        body = kernel
        extra_specs = [each((tokens, 256))]
        extra_shapes = [shape_of(BF16, micro, tokens, 256)]
    return pl.pallas_call(
        body,
        grid=(micro,),
        in_specs=[each((rows, 256)), whole(weights.shape), whole(vectors.shape)],
        out_specs=[
            each((tokens, 256)),
            each((tokens, 128)),
            each((tokens, 128)),
            each((tokens, 128)),
            each((rows, 128)),
        ] + extra_specs,
        out_shape=[
            shape_of(BF16, micro, tokens, 256),
            shape_of(BF16, micro, tokens, 128),
            shape_of(BF16, micro, tokens, 128),
            shape_of(F32, micro, tokens, 128),
            shape_of(BF16, micro, rows, 128),
        ] + extra_shapes,
        scratch_shapes=scratch,
        compiler_params=PARAMS,
        name="attention_forward_%d" % half,
    )(x, weights, vectors)


def middle_call(x, att_h, att_v, top, nb, length, weights, vectors):
    micro, tokens, _ = x.shape
    packed = nb * PIECE

    def kernel(
        x_ref, h_ref, v_ref, top_ref, w_ref, vec_ref,
        out_ref, gm_ref, gh_ref, gv_ref, gp_ref, g1_ref, g2_ref, rows_ref,
        hot_in, hot_out, att, n2, acc, gn,
    ):
        @pl.when(pl.program_id(0) == 0)
        def _():
            hot_in[...] = order_in(nb, length)
            hot_out[...] = order_out(nb, length)
            for ref in (gp_ref, g1_ref, g2_ref, rows_ref):
                ref[...] = jnp.zeros_like(ref)

        att[:, 0:128] = h_ref[...]
        att[:, 128:256] = mm(hot_in[...], v_ref[...]).astype(BF16)
        out, grad_middle, grad_att = feed_forward(
            x_ref[...].astype(F32), att[...], top_ref[...], w_ref, ROW_PROJ, vec_ref, n2, acc, gn, gp_ref, g1_ref, g2_ref, rows_ref
        )
        out_ref[...] = out
        gm_ref[...] = grad_middle
        gh_ref[...] = grad_att[:, 0:128]
        gv_ref[...] = mm(hot_out[...], grad_att[:, 128:256]).astype(BF16)

    return pl.pallas_call(
        kernel,
        grid=(micro,),
        in_specs=[
            each((tokens, 256)), each((tokens, 128)), each((packed, 128)), each((tokens, 256)),
            whole(weights.shape), whole(vectors.shape),
        ],
        out_specs=[
            each((tokens, 256)), each((tokens, 256)), each((tokens, 128)), each((packed, 128)),
            whole((256, 256)), whole((256, 1024)), whole((256, 1024)), whole((8, 256)),
        ],
        out_shape=[
            shape_of(BF16, micro, tokens, 256), shape_of(F32, micro, tokens, 256),
            shape_of(BF16, micro, tokens, 128), shape_of(BF16, micro, packed, 128),
            shape_of(F32, 256, 256), shape_of(F32, 256, 1024), shape_of(F32, 256, 1024), shape_of(F32, 8, 256),
        ],
        scratch_shapes=[
            pltpu.VMEM((tokens, packed), BF16), pltpu.VMEM((packed, tokens), BF16),
            pltpu.VMEM((tokens, 256), BF16), pltpu.VMEM((tokens, 256), BF16),
            pltpu.VMEM((tokens, 256), F32), pltpu.VMEM((tokens, 256), F32),
        ],
        compiler_params=PARAMS,
        name="feed_forward",
    )(x, att_h, att_v, top, weights, vectors)


def backward_call(x, grad, qa, k, v, o, half, nb, length, weights, vectors):
    micro, tokens, _ = x.shape
    packed = nb * PIECE

    def kernel(
        x_ref, g_ref, qa_ref, k_ref, v_ref, o_ref, w_ref, vec_ref, gn_ref, gw_ref, rows_ref,
        da, dq, dk, dv, *scr,
    ):
        @pl.when(pl.program_id(0) == 0)
        def _():
            gw_ref[...] = jnp.zeros_like(gw_ref)
            rows_ref[...] = jnp.zeros_like(rows_ref)
            if half == 1:
                scr[0][...] = order_in(nb, length)
                scr[1][...] = order_out(nb, length)

        grad_in = g_ref[...] if half == 0 else mm(scr[0][...], g_ref[...]).astype(BF16)
        part = attention_backward(
            x_ref[...].astype(F32), half, length, grad_in, lane_blocks(w_ref, half), vec_ref, qa_ref, k_ref, v_ref, o_ref,
            da, dq, dk, dv, gw_ref, rows_ref,
        )
        if half == 0:
            gn_ref[...] = part
        else:
            gn_ref[...] = mm(scr[1][...], part.astype(BF16)).astype(BF16)

    rows = tokens if half == 0 else packed
    scratch = [
        pltpu.VMEM((tokens, 256), BF16), pltpu.VMEM((128, tokens), F32),
        pltpu.VMEM((tokens, 128), F32), pltpu.VMEM((tokens, 128), F32),
    ]
    if half == 1:
        scratch += [pltpu.VMEM((tokens, packed), BF16), pltpu.VMEM((packed, tokens), BF16)]
    return pl.pallas_call(
        kernel,
        grid=(micro,),
        in_specs=[
            each((tokens, 256)), each((rows, 128)), each((tokens, 256)), each((tokens, 128)),
            each((tokens, 128)), each((tokens, 128)), whole(weights.shape), whole(vectors.shape),
        ],
        out_specs=[each((rows, 256)), whole((256, 384)), whole((16, 128))],
        out_shape=[
            shape_of(F32 if half == 0 else BF16, micro, rows, 256),
            shape_of(F32, 256, 384), shape_of(F32, 16, 128),
        ],
        scratch_shapes=scratch,
        compiler_params=PARAMS,
        name="attention_backward_%d" % half,
    )(x, grad, qa, k, v, o, weights, vectors)


def last_call(x, grad_middle, part_h, part_v, nb, length, vectors):
    micro, tokens, _ = x.shape
    packed = nb * PIECE

    def kernel(x_ref, gm_ref, h_ref, v_ref, vec_ref, out_ref, hot_in):
        @pl.when(pl.program_id(0) == 0)
        def _():
            hot_in[...] = order_in(nb, length)

        grad_normed = h_ref[...] + mm(hot_in[...], v_ref[...])
        unit, inverse = unit_rows(x_ref[...].astype(F32))
        out_ref[...] = (
            gm_ref[...] + norm_back(grad_normed, vec_ref[0:1], unit, inverse)
        ).astype(BF16)

    return pl.pallas_call(
        kernel,
        grid=(micro,),
        in_specs=[
            each((tokens, 256)), each((tokens, 256)), each((tokens, 256)), each((packed, 256)), whole(vectors.shape),
        ],
        out_specs=each((tokens, 256)),
        out_shape=shape_of(BF16, micro, tokens, 256),
        scratch_shapes=[pltpu.VMEM((tokens, packed), BF16)],
        compiler_params=PARAMS,
        name="input_gradient",
    )(x, grad_middle, part_h, part_v, vectors)


def repeat(lo, hi, body):
    def step(k, c):
        body(k)
        return c

    lax.fori_loop(lo, hi, step, 0)


def remote(src, dst, ss, rs, dev):
    return pltpu.make_async_remote_copy(
        src_ref=src, dst_ref=dst, send_sem=ss, recv_sem=rs, device_id=dev, device_id_type=MESH
    )


class Swap:
    def __init__(self, n, out_ref, in_ref, send_sem, recv_sem):
        self.n, self.out, self.into, self.ss, self.rs = n, out_ref, in_ref, send_sem, recv_sem
        self.me = lax.axis_index("band")

    def rows(self, i):
        return pl.ds(pl.multiple_of(i * PIECE, PIECE), PIECE)

    def send(self, m):
        mine = self.rows(self.me)

        def one(k):
            d = lax.rem(self.me + k, self.n)
            remote(
                self.out.at[m, self.rows(d)],
                self.into.at[m, mine],
                self.ss.at[m, k],
                self.rs.at[m, k],
                {"band": d},
            ).start()

        repeat(1, self.n, one)
        self.into[m, mine, :] = self.out[m, mine, :]

    def wait(self, m):
        def one(k):
            s = lax.rem(self.me - k + self.n, self.n)
            remote(
                self.out.at[m, self.rows(s)],
                self.into.at[m, self.rows(s)],
                self.ss.at[m, k],
                self.rs.at[m, k],
                {"band": s},
            ).wait()

        repeat(1, self.n, one)


class Sum:
    def __init__(self, nb, nx, x_ref, o_ref, got, half, recv, sems):
        self.nx = nx
        self.nq = (nb // 2) * nx
        self.p = x_ref.shape[0] // (2 * self.nq)
        band = lax.axis_index("band")
        self.core = lax.rem(band, 2)
        self.q = (band // 2) * nx + lax.axis_index("batch")
        self.sibling = {"band": band + 1 - 2 * self.core}
        self.x, self.o, self.got, self.half, self.recv = x_ref, o_ref, got, half, recv
        self.sems = sems

    def chip(self, t):
        return {"band": (t // self.nx) * 2 + self.core, "batch": lax.rem(t, self.nx)}

    def ahead(self, k):
        return lax.rem(self.q + k, self.nq)

    def behind(self, k):
        return lax.rem(self.q - k + self.nq, self.nq)

    def wide(self, c, t):
        return pl.ds(pl.multiple_of((c * self.nq + t) * self.p, 16), self.p)

    def thin(self, t):
        return pl.ds(pl.multiple_of(t * self.p, 16), self.p)

    def sem(self, i, k):
        return self.sems.at[2 * i, k], self.sems.at[2 * i + 1, k]

    def pair_copy(self, k, side):
        t = self.ahead(k)
        return remote(
            self.x.at[self.wide(side, t)], self.got.at[self.thin(t)], *self.sem(0, t), self.sibling
        )

    def start(self):
        repeat(1, self.nq + 1, lambda k: self.pair_copy(k, 1 - self.core).start())

    def scatter(self):
        def one(k):
            t = self.ahead(k)
            self.pair_copy(k, self.core).wait()
            self.half[self.thin(t)] = (
                self.x[self.wide(self.core, t)].astype(F32) + self.got[self.thin(t)].astype(F32)
            ).astype(BF16)

            @pl.when(k < self.nq)
            def _():
                remote(
                    self.half.at[self.thin(t)],
                    self.recv.at[self.thin(self.q)],
                    *self.sem(1, k),
                    self.chip(t),
                ).start()

        repeat(1, self.nq + 1, one)

    def gather(self):
        def one(k, acc):
            t = self.behind(k)
            remote(
                self.half.at[self.thin(t)],
                self.recv.at[self.thin(t)],
                *self.sem(1, k),
                self.chip(t),
            ).wait()
            return acc + self.recv[self.thin(t)].astype(F32)

        total = lax.fori_loop(1, self.nq, one, self.half[self.thin(self.q)].astype(F32))
        mine = self.wide(self.core, self.q)
        self.o[mine] = total.astype(BF16)

        def give(k):
            remote(
                self.o.at[mine], self.o.at[mine], *self.sem(2, k), self.chip(self.ahead(k))
            ).start()

        repeat(1, self.nq, give)
        self.pass_on(self.q, self.core).start()

    def pass_on(self, t, side):
        return remote(
            self.o.at[self.wide(self.core, t)],
            self.o.at[self.wide(side, t)],
            *self.sem(3, t),
            self.sibling,
        )

    def relay(self):
        mine = self.wide(self.core, self.q)

        def one(k):
            t = self.behind(k)
            remote(
                self.o.at[mine], self.o.at[self.wide(self.core, t)], *self.sem(2, k), self.chip(t)
            ).wait()
            self.pass_on(t, self.core).start()

        repeat(1, self.nq, one)

    def finish(self):
        repeat(0, self.nq, lambda t: self.pass_on(t, 1 - self.core).wait())


ROWS_A = 1536
ROWS_B = 2304
ROWS_G = 800


def up(rows, unit):
    return -(-rows // unit) * unit


def split_rows(ref, at, rows):
    n = rows.shape[0]
    high = rows.astype(BF16)
    ref[at : at + n, :] = high
    ref[at + n : at + 2 * n, :] = (rows - high.astype(F32)).astype(BF16)


def block_kernel(
    nb, nx, length,
    own_ref, x_ref, top_ref, wq_ref, wp_ref, w1_ref, w2_ref, vec_ref,
    out_ref, ing_ref, gb_ref, gav_ref, gah_ref,
    wa_in, wb_in, wa, wb, gb_in, gav_in, gah_in,
    wide_got, wide_half, wide_recv, a_got, a_half, a_recv,
    gb_got, gb_half, gb_recv, v_got, v_half, v_recv, h_got, h_half, h_recv,
    hot_in, hot_out, x_out, x_in, a_out, a_in, g_out, g_in, p_out, p_in,
    xs, qa, ks, vs, os, vx, att, n2, acc, gn, gm, grad_h, part_h,
    gp, g1, g2, rows_mid, gw_v, gw_h, rows_v, rows_h, da, dq, dk, dv,
    x_ss, x_rs, a_ss, a_rs, g_ss, g_rs, p_ss, p_rs,
    wa_sem, wb_sem, gb_sem, gav_sem, gah_sem,
):
    band = lax.axis_index("band")
    batch = lax.axis_index("batch")
    device = band * nx + batch
    micro = x_ref.shape[0]
    core = lax.rem(band, 2)
    bar = pltpu.get_barrier_semaphore()
    repeat(
        1,
        nb,
        lambda k: pl.semaphore_signal(
            bar, inc=1, device_id={"band": lax.rem(band + k, nb)}, device_id_type=MESH
        ),
    )

    def greet(t):
        other = lax.rem(batch + 1 + t // (nb // 2), nx)
        pl.semaphore_signal(
            bar,
            inc=1,
            device_id={"band": lax.rem(t, nb // 2) * 2 + core, "batch": other},
            device_id_type=MESH,
        )

    repeat(0, (nb // 2) * (nx - 1), greet)

    sum_wa = Sum(nb, nx, wa_in, wa, a_got, a_half, a_recv, wa_sem)
    sum_wb = Sum(nb, nx, wb_in, wb, wide_got, wide_half, wide_recv, wb_sem)
    sum_gb = Sum(nb, nx, gb_in, gb_ref, gb_got, gb_half, gb_recv, gb_sem)
    sum_gav = Sum(nb, nx, gav_in, gav_ref, v_got, v_half, v_recv, gav_sem)
    sum_gah = Sum(nb, nx, gah_in, gah_ref, h_got, h_half, h_recv, gah_sem)
    swap_x = Swap(nb, x_out, x_in, x_ss, x_rs)
    swap_a = Swap(nb, a_out, a_in, a_ss, a_rs)
    swap_g = Swap(nb, g_out, g_in, g_ss, g_rs)
    swap_p = Swap(nb, p_out, p_in, p_ss, p_rs)

    def own(ref, which, cols):
        return jnp.where(own_ref[which] == device, ref[0, :, cols], 0.0).astype(BF16)

    for b in range(6):
        wa_in[256 * b : 256 * b + 256, :] = own(wq_ref, 0, slice(128 * b, 128 * b + 128))
    if wa_in.shape[0] > ROWS_A:
        wa_in[ROWS_A:, :] = jnp.zeros((wa_in.shape[0] - ROWS_A, 128), BF16)
    pl.semaphore_wait(bar, nb - 1 + (nb // 2) * (nx - 1))
    sum_wa.start()
    wb_in[0:256, :] = own(wp_ref, 1, slice(0, 256))
    for f in range(4):
        wb_in[256 * (f + 1) : 256 * (f + 2), :] = own(w1_ref, 2, slice(256 * f, 256 * f + 256))
    wb_in[1280:ROWS_B, :] = own(w2_ref, 3, slice(0, 256))
    wb_in[ROWS_B:, :] = jnp.zeros((wb_in.shape[0] - ROWS_B, 256), BF16)
    sum_wa.scatter()
    hot_out[...] = order_out(nb, length)
    x_out[0] = mm(hot_out[...], x_ref[0]).astype(BF16)
    swap_x.send(0)
    sum_wa.gather()
    hot_in[...] = order_in(nb, length)
    for m in range(1, micro):
        x_out[m] = mm(hot_out[...], x_ref[m]).astype(BF16)
        swap_x.send(m)
    sum_wb.start()
    for ref in (gp, g1, g2, rows_mid, gw_v, gw_h, rows_v, rows_h):
        ref[...] = jnp.zeros_like(ref)
    sum_wa.relay()
    sum_wa.finish()

    def blocks(half):
        return lambda b: wa[256 * (2 * b + half) : 256 * (2 * b + half) + 256, :]

    def forward_h(m):
        attention_forward(
            x_ref[m].astype(F32), 0, length, blocks(0), vec_ref,
            qa.at[m], ks.at[m], vs.at[m], os.at[m], att.at[m, :, pl.ds(0, 128)], vx,
        )

    def forward_v(m):
        swap_x.wait(m)
        xs[m] = mm(hot_in[...], x_in[m]).astype(BF16)
        w = micro + m
        attention_forward(
            xs[m].astype(F32), 1, length, blocks(1), vec_ref,
            qa.at[w], ks.at[w], vs.at[w], os.at[w], att.at[m, :, pl.ds(128, 128)], vx,
        )
        a_out[m] = mm(hot_out[...], att[m, :, 128:256]).astype(BF16)
        swap_a.send(m)

    def forward_step(i):
        @pl.when((i == 0) | (i > micro))
        def _():
            forward_h(jnp.where(i == 0, 0, i - micro))

        @pl.when((i > 0) & (i <= micro))
        def _():
            forward_v(i - 1)

        @pl.when(i == 0)
        def _():
            sum_wb.scatter()

        @pl.when(i == 1)
        def _():
            sum_wb.gather()

        @pl.when(i == 2)
        def _():
            sum_wb.relay()

    repeat(0, 2 * micro, forward_step)
    sum_wb.finish()

    def middle_step(m):
        swap_a.wait(m)
        att[m, :, 128:256] = mm(hot_in[...], a_in[m]).astype(BF16)
        out, grad_middle, grad_att = feed_forward(
            x_ref[m].astype(F32), att[m], top_ref[m], wb, 0, vec_ref, n2, acc, gn,
            gp, g1, g2, rows_mid,
        )
        out_ref[m] = out
        gm[m] = grad_middle
        grad_h[m] = grad_att[:, 0:128]
        g_out[m] = mm(hot_out[...], grad_att[:, 128:256]).astype(BF16)
        swap_g.send(m)

    repeat(0, micro, middle_step)
    gb_in[0:256, :] = jnp.transpose(gp[...]).astype(BF16)
    for f in range(4):
        cols = slice(256 * f, 256 * f + 256)
        gb_in[256 * (f + 1) : 256 * (f + 2), :] = g1[:, cols].astype(BF16)
        gb_in[1280 + 256 * f : 1536 + 256 * f, :] = jnp.transpose(g2[:, cols]).astype(BF16)
    gb_in[ROWS_B:, :] = jnp.zeros((gb_in.shape[0] - ROWS_B, 256), BF16)
    split_rows(gb_in, ROWS_B, rows_mid[...])
    sum_gb.start()

    def backward_v(m):
        swap_g.wait(m)
        w = micro + m
        grad_in = mm(hot_in[...], g_in[m]).astype(BF16)
        part = attention_backward(
            xs[m].astype(F32), 1, length, grad_in, blocks(1), vec_ref,
            qa.at[w], ks.at[w], vs.at[w], os.at[w], da, dq, dk, dv, gw_v, rows_v,
        )
        p_out[m] = mm(hot_out[...], part.astype(BF16)).astype(BF16)
        swap_p.send(m)

        @pl.when(m == 0)
        def _():
            sum_gb.scatter()

    repeat(0, micro, backward_v)
    sum_gb.gather()

    def fill(ref, gw, rows):
        for b in range(3):
            ref[256 * b : 256 * b + 256, :] = gw[:, 128 * b : 128 * b + 128].astype(BF16)
        split_rows(ref, 768, rows[...])
        ref[ROWS_G:, :] = jnp.zeros((ref.shape[0] - ROWS_G, 128), BF16)

    fill(gav_in, gw_v, rows_v)
    sum_gav.start()

    def backward_h(m):
        part_h[m] = attention_backward(
            x_ref[m].astype(F32), 0, length, grad_h[m], blocks(0), vec_ref,
            qa.at[m], ks.at[m], vs.at[m], os.at[m], da, dq, dk, dv, gw_h, rows_h,
        )

        @pl.when(m == 0)
        def _():
            sum_gb.relay()
            sum_gav.scatter()

    repeat(0, micro, backward_h)
    fill(gah_in, gw_h, rows_h)
    sum_gah.start()
    sum_gav.gather()
    sum_gb.finish()
    sum_gah.scatter()

    def last_step(m):
        swap_p.wait(m)
        grad_normed = part_h[m] + mm(hot_in[...], p_in[m])
        unit, inverse = unit_rows(x_ref[m].astype(F32))
        ing_ref[m] = (gm[m] + norm_back(grad_normed, vec_ref[0:1], unit, inverse)).astype(BF16)

    last_step(0)
    sum_gah.gather()
    sum_gav.relay()
    repeat(1, micro, last_step)
    sum_gah.relay()
    sum_gav.finish()
    sum_gah.finish()


def block_call(x, top, owners, w_qkv, w_proj, w_fc1, w_fc2, vectors, nb, nx, length):
    micro, tokens, _ = x.shape
    packed = nb * PIECE
    nq = nb // 2 * nx
    unit = 32 * nq
    ra, rb, rg = up(ROWS_A, unit), up(ROWS_B + 16, unit), up(ROWS_G, unit)
    vm = pltpu.VMEM
    windows = 2 * micro

    def steps(rows, cols):
        return [vm((rows // 2, cols), BF16)] * 3

    scratch = (
        [vm((ra, 128), BF16), vm((rb, 256), BF16), vm((ra, 128), BF16), vm((rb, 256), BF16)]
        + [vm((rb, 256), BF16), vm((rg, 128), BF16), vm((rg, 128), BF16)]
        + steps(rb, 256) + steps(ra, 128) + steps(rb, 256) + steps(rg, 128) + steps(rg, 128)
        + [vm((tokens, packed), BF16), vm((packed, tokens), BF16)]
        + [vm((micro, packed, 256), BF16)] * 2
        + [vm((micro, packed, 128), BF16)] * 4
        + [vm((micro, packed, 256), BF16)] * 2
        + [
            vm((micro, tokens, 256), BF16),
            vm((windows, tokens, 256), BF16),
            vm((windows, tokens, 128), BF16),
            vm((windows, tokens, 128), BF16),
            vm((windows, tokens, 128), F32),
            vm((tokens, 256), BF16),
            vm((micro, tokens, 256), BF16),
            vm((tokens, 256), BF16),
            vm((tokens, 256), F32),
            vm((tokens, 256), F32),
            vm((micro, tokens, 256), F32),
            vm((micro, tokens, 128), BF16),
            vm((micro, tokens, 256), F32),
            vm((256, 256), F32),
            vm((256, 1024), F32),
            vm((256, 1024), F32),
            vm((8, 256), F32),
            vm((256, 384), F32),
            vm((256, 384), F32),
            vm((16, 128), F32),
            vm((16, 128), F32),
            vm((tokens, 256), BF16),
            vm((128, tokens), F32),
            vm((tokens, 128), F32),
            vm((tokens, 128), F32),
        ]
        + [pltpu.SemaphoreType.DMA((micro, nb))] * 8
        + [pltpu.SemaphoreType.DMA((8, nq))] * 5
    )
    whole_vmem = pl.BlockSpec(memory_space=vm)
    return pl.pallas_call(
        functools.partial(block_kernel, nb, nx, length),
        in_specs=[pl.BlockSpec(memory_space=pltpu.SMEM)] + [whole_vmem] * 7,
        out_specs=[whole_vmem] * 5,
        out_shape=[
            shape_of(BF16, micro, tokens, 256), shape_of(BF16, micro, tokens, 256),
            shape_of(BF16, rb, 256), shape_of(BF16, rg, 128), shape_of(BF16, rg, 128),
        ],
        scratch_shapes=scratch,
        compiler_params=pltpu.CompilerParams(
            collective_id=0, has_side_effects=True, vmem_limit_bytes=VMEM_LIMIT
        ),
        name="block",
    )(owners, x, top, w_qkv, w_proj, w_fc1, w_fc2, vectors)


def parts_of(a):
    high = a.astype(BF16)
    return high, (a - high.astype(F32)).astype(BF16)


def careful(op, a, b):
    ah, al = parts_of(a)
    bh, bl = parts_of(b)
    return op(ah, bh) + (op(ah, bl) + op(al, bh))


def adam_kernel(
    vrows, rows,
    own_ref, gb_ref, gav_ref, gah_ref, vec_ref, vf_ref, vs_ref, *refs,
):
    moments = refs[0:12]
    bases = refs[12:20]
    grads = refs[20:24]
    outs = refs[24:36]
    vg_ref, vfn_ref, vsn_ref, vn_ref = refs[36:40]
    held = refs[40:52]
    left = refs[52:60]
    zeros_ref, in_sem, out_sem = refs[60:63]
    device = lax.axis_index("band") * lax.axis_size("batch") + lax.axis_index("batch")
    is_own = [own_ref[i] == device for i in range(4)]

    def load(i):
        pairs = [(moments[3 * i + j].at[0], held[3 * i + j], 5 * i + j) for j in range(3)]
        pairs += [(bases[2 * i + j], left[2 * i + j], 5 * i + 3 + j) for j in range(2)]
        return [pltpu.make_async_copy(a, b, in_sem.at[s]) for a, b, s in pairs]

    def store(i):
        return [
            pltpu.make_async_copy(held[3 * i + j], outs[3 * i + j].at[0], out_sem.at[3 * i + j])
            for j in range(3)
        ]

    def blank(i):
        copies = []
        for j in range(3):
            shape = outs[3 * i + j].shape
            copies.append(
                pltpu.make_async_copy(
                    zeros_ref.at[pl.ds(0, shape[1]), pl.ds(0, shape[2])],
                    outs[3 * i + j].at[0],
                    out_sem.at[3 * i + j],
                )
            )
        return copies

    for i in range(4):
        @pl.when(is_own[i])
        def _():
            for c in load(i):
                c.start()

    zeros_ref[...] = jnp.zeros_like(zeros_ref)
    for i in range(4):
        @pl.when(jnp.logical_not(is_own[i]))
        def _():
            for c in blank(i):
                c.start()

    for b in range(3):
        for half, ref in ((0, gah_ref), (1, gav_ref)):
            at = 256 * b + 128 * half
            grads[0][:, at : at + 128] = ref[256 * b : 256 * b + 256, :].astype(F32)
    grads[1][...] = gb_ref[0:256, :].astype(F32)
    for f in range(4):
        grads[2][:, 256 * f : 256 * f + 256] = gb_ref[256 * (f + 1) : 256 * (f + 2), :].astype(F32)
    grads[3][...] = gb_ref[1280:ROWS_B, :].astype(F32)

    mid = gb_ref[ROWS_B : ROWS_B + 8, :].astype(F32) + gb_ref[ROWS_B + 8 : ROWS_B + 16, :].astype(F32)
    side = [r[768:784, :].astype(F32) + r[784:800, :].astype(F32) for r in (gah_ref, gav_ref)]
    both = side[0] + side[1]
    for i in range(2):
        vg_ref[0:1, 128 * i : 128 * i + 128] = both[12 + i : 13 + i]
        vg_ref[1:2, 128 * i : 128 * i + 128] = both[14 + i : 15 + i]
        vg_ref[2:4, 128 * i : 128 * i + 128] = side[i][0:2]
        vg_ref[12:22, 128 * i : 128 * i + 128] = side[i][2:12]
    vg_ref[4:12, :] = mid
    grad = vg_ref[...]
    first_new = BETA_ONE * vf_ref[...] + (1.0 - BETA_ONE) * grad
    second_new = BETA_TWO * vs_ref[...] + (1.0 - BETA_TWO) * grad * grad
    vfn_ref[...] = first_new
    vsn_ref[...] = second_new
    vn_ref[...] = vec_ref[...] - RATE_VECTORS * (first_new / (1.0 - BETA_ONE**STEP)) / (
        jnp.sqrt(second_new / (1.0 - BETA_TWO**STEP)) + EPS_ADAM
    )

    for i in range(4):
        @pl.when(is_own[i])
        def _():
            for c in load(i):
                c.wait()
            first, second, weight = held[3 * i], held[3 * i + 1], held[3 * i + 2]
            lb, rb = left[2 * i], left[2 * i + 1]
            g = grads[i][...].astype(BF16)
            lh, ll = parts_of(lb[...])
            if i == 3:
                once = jnp.transpose(mm_tn(g, lh) + mm_tn(g, ll))
            else:
                once = mm_tn(lh, g) + mm_tn(ll, g)
            turned = careful(mm, once, rb[...])
            first_new = BETA_ONE * first[...] + (1.0 - BETA_ONE) * turned
            second_new = BETA_TWO * second[...] + (1.0 - BETA_TWO) * turned * turned
            first[...] = first_new
            second[...] = second_new
            step = (first_new / (1.0 - BETA_ONE**STEP)) / (
                jnp.sqrt(second_new / (1.0 - BETA_TWO**STEP)) + EPS_ADAM
            )
            back = mm_nt(mm(lh, step.astype(BF16)).astype(BF16), rb[...].astype(BF16))
            weight[...] = weight[...] - RATE * back - RATE * DECAY * weight[...]
            for c in store(i):
                c.start()

    for i in range(4):
        for c in store(i):
            c.wait()


def adam_call(owners, gb, gav, gah, vectors, vectors_first, vectors_second, slots, bases):
    vm = pltpu.VMEM
    any_space = pl.BlockSpec(memory_space=pl.ANY)
    vspec = pl.BlockSpec(memory_space=vm)
    sizes = [(s.shape[1], s.shape[2]) for s in slots[::3]]
    vshape = shape_of(F32, *vectors.shape)
    tallest = max(a for a, _ in sizes)
    widest = max(b for _, b in sizes)
    return pl.pallas_call(
        functools.partial(adam_kernel, vectors.shape[0], None),
        in_specs=[pl.BlockSpec(memory_space=pltpu.SMEM)] + [vspec] * 6 + [any_space] * 20,
        out_specs=[vspec] * 4 + [any_space] * 12 + [vspec] * 4,
        out_shape=[shape_of(F32, *s) for s in sizes]
        + [shape_of(F32, *s.shape) for s in slots]
        + [vshape] * 4,
        scratch_shapes=[vm((s.shape[1], s.shape[2]), F32) for s in slots]
        + [vm(b.shape, F32) for b in bases]
        + [vm((tallest, widest), F32), pltpu.SemaphoreType.DMA((20,)), pltpu.SemaphoreType.DMA((12,))],
        compiler_params=pltpu.CompilerParams(vmem_limit_bytes=VMEM_LIMIT),
        name="adam",
    )(owners, gb, gav, gah, vectors, vectors_first, vectors_second, *slots, *bases)


def wide_to_stack(w):
    n = w.shape[1] // 256
    return w.reshape(256, n, 256).transpose(1, 0, 2).reshape(256 * n, 256)


def by_steps(x, top, owners, slots, vectors, nb, nx, length):
    device_index = lax.axis_index(("band", "batch"))

    def own(slot, which):
        return jnp.where(device_index == owners[which], slot[0], 0.0).astype(BF16)

    stacked = jnp.concatenate(
        [
            wide_to_stack(own(slots[0], 0)),
            own(slots[1], 1),
            wide_to_stack(own(slots[2], 2)),
            own(slots[3], 3),
        ],
        axis=0,
    )
    weights = sum_everywhere(stacked, nb, nx, 0)[:ROW_END]

    def swap(packed, cid):
        m, rows, ch = packed.shape
        swapped = packed.reshape(m, nb, PIECE, ch).transpose(1, 0, 2, 3).reshape(m * rows, ch)
        got = exchange(swapped, nb, cid)
        return got.reshape(nb, m, PIECE, ch).transpose(1, 0, 2, 3).reshape(m, rows, ch)

    columns = swap(pack_tokens(x, nb, length), 1)
    qa_v, k_v, v_v, o_v, att_v, x_v = forward_call(columns, 1, nb, length, weights, vectors)
    qa_h, k_h, v_h, o_h, att_h = forward_call(x, 0, nb, length, weights, vectors)
    att_v = swap(att_v, 2)
    block_out, grad_middle, grad_h, grad_v, gp_t, g1, g2_t, rows_mid = middle_call(
        x, att_h, att_v, top, nb, length, weights, vectors
    )
    grad_v = swap(grad_v, 3)
    part_v, gw_v, rows_v = backward_call(
        x_v, grad_v, qa_v, k_v, v_v, o_v, 1, nb, length, weights, vectors
    )
    part_h, gw_h, rows_h = backward_call(
        x, grad_h, qa_h, k_h, v_h, o_h, 0, nb, length, weights, vectors
    )
    part_v = swap(part_v, 4)
    input_grad = last_call(x, grad_middle, part_h, part_v, nb, length, vectors)

    def two(rows):
        high = rows.astype(BF16)
        return [high, (rows - high.astype(F32)).astype(BF16)]

    gb = jnp.concatenate(
        [gp_t.T.astype(BF16), wide_to_stack(g1.astype(BF16)), g2_t.T.astype(BF16)] + two(rows_mid),
        axis=0,
    )

    def side(gw, rows):
        return jnp.concatenate(
            [gw[:, 128 * b : 128 * b + 128].astype(BF16) for b in range(3)] + two(rows), axis=0
        )

    gb = sum_everywhere(gb, nb, nx, 5)
    gav = sum_everywhere(side(gw_v, rows_v), nb, nx, 6)
    gah = sum_everywhere(side(gw_h, rows_h), nb, nx, 7)
    return block_out, input_grad, gb, gav, gah


def per_device(
    tokens_in, cotangent, owners,
    weight_qkv, weight_proj, weight_fc1, weight_fc2,
    first_qkv, second_qkv, first_proj, second_proj, first_fc1, second_fc1, first_fc2, second_fc2,
    left_qkv, right_qkv, left_proj, right_proj, left_fc1, right_fc1, left_fc2, right_fc2,
    vectors, vectors_first, vectors_second,
    *, nb, nx,
):
    micro, images, band_rows, length, channels = tokens_in.shape
    tokens = band_rows * length
    x = tokens_in.reshape(micro * images, tokens, channels)
    top = cotangent.reshape(micro * images, tokens, channels)
    weights = (weight_qkv, weight_proj, weight_fc1, weight_fc2)
    if tokens <= 1024:
        block_out, input_grad, gb, gav, gah = block_call(
            x, top, owners, *weights, vectors, nb, nx, length
        )
    else:
        block_out, input_grad, gb, gav, gah = by_steps(
            x, top, owners, weights, vectors, nb, nx, length
        )
    slots = (
        first_qkv, second_qkv, weight_qkv, first_proj, second_proj, weight_proj,
        first_fc1, second_fc1, weight_fc1, first_fc2, second_fc2, weight_fc2,
    )
    bases = (left_qkv, right_qkv, left_proj, right_proj, left_fc1, right_fc1, left_fc2, right_fc2)
    done = adam_call(
        owners, gb, gav, gah, vectors, vectors_first, vectors_second, slots, bases
    )
    results = [block_out.reshape(tokens_in.shape), input_grad.reshape(tokens_in.shape)]
    for i in range(4):
        results.append(done[i])
        results += list(done[4 + 3 * i : 7 + 3 * i])
    return tuple(results) + tuple(done[16:20])


def solution(mesh):
    tokens_spec = P(None, "batch", "band", None, None)
    slot_spec = P(("band", "batch"), None, None)
    return jax.shard_map(
        functools.partial(per_device, nb=mesh.shape["band"], nx=mesh.shape["batch"]),
        mesh=mesh,
        in_specs=(tokens_spec, tokens_spec, P()) + (slot_spec,) * 12 + (P(),) * 11,
        out_specs=(tokens_spec, tokens_spec)
        + (P(), slot_spec, slot_spec, slot_spec) * 4
        + (P(),) * 4,
        check_vma=False,
    )
```

time: 754 us -> 225 us (0.30); the launches traced: 746 us -> 224 us
  Pallas kernels: 0 us -> 222 us
  waiting for transfers between devices: 169 us -> 0 us
  matrix products: 156 us -> 0 us
  blocking collectives: 121 us -> 0 us
  local copies, waits for them, and re-layouts: 121 us -> 1.78 us
  other arithmetic: 115 us -> 0 us
  starting transfers between devices: 42.5 us -> 0 us
  between operations: 20.4 us -> 0.7 us
    pallas_call x0 -> x2, Pallas kernels: none -> 222 us  [the longest x1 210 us: block_call(): pl.pallas_call(functools.partial(block_kernel, nb, nx, length), in_specs=...]
    dot_general x52 -> x0, matrix products: 156 us -> none  [the longest x4 23.3 us: attend_backward(): jnp.einsum('hqk,qhd->khd', softmax_f.astype(jnp.bfloat16), grad_h, prefer...]
    psum x1 -> x0, waiting for transfers between devices: 135 us -> none  [per_device(): lax.psum((totals[0], totals[1], totals[2], totals[3], totals[4]), ('band'...]
    psum x2 -> x0, blocking collectives: 121 us -> none  [the longest x1 80.7 us: per_device(): lax.psum((own_slot(weight_qkv, owners[0], device_index), own_slot(weight_...]
    all_to_all x8 -> x0, starting transfers between devices: 42.1 us -> none  [the longest x2 12.5 us: per_device(): lax.all_to_all(grad_vert.reshape(images_n, rows_all, stripe_cols, 3 * hal...]
    unnamed x492 -> x6, local copies, waits for them, and re-layouts: 40.7 us -> 1.78 us
    convert_element_type x13 -> x0, other arithmetic: 36.7 us -> none  [the longest x4 20.7 us: attend_backward(): grad_scores = (softmax_f * (grad_soft - inner_sum)).astype(jnp.bfloat16)]
    reduce_sum x20 -> x0, other arithmetic: 35.8 us -> none  [the longest x6 18.6 us: position_conv(): padded[:, row_off:row_off + rows_n, col_off:col_off + cols_n, :]]
  transfers between devices with their start and end apart: 9 -> 0, of which waited for: 5 -> 0; matrix products, arithmetic and copies ran while one was open for 20% -> 0% of each run, Pallas kernels for 0% -> 0%
where the time goes in v1:
time: 225 us; the launch traced here: 224 us
  Pallas kernels  222 us (99%)
    pallas_call x1, Pallas kernels, block_call(): pl.pallas_call(functools.partial(block_kernel, nb, nx, length), in_specs=...  210 us
    pallas_call x1, Pallas kernels, adam_call(): pl.pallas_call(functools.partial(adam_kernel, vectors.shape[0], None), in...  12.1 us

profile of v1, /device:TPU:0, one launch (start us, length us, event | category | flops | bytes accessed | tf_op | source)
XLA Modules:
  0.0 224.5 jit_solution(18381574655526372663)
XLA Ops:
  0.7 209.9 %block.1 = (bf16[2,784,256]{2,1,0:T(8,128)(2,1)}, bf16[2,784,256]{2,1,0:T(8,128)(2,1)}, bf16[2560,256]{1,0:T(8,128)(2,1)}, bf16[1024,128]{1,0:T(8,128)(2,1)}, bf16[1024,128]{1,0:T(8,128)(2,1)}) custom-call(s32[4]{0:T(128)} %own_ref.3, bf16[2,784,256]{2,1,0:T(8,128)(2,1)} %bitcast.8, bf16[2,784,256]{2,1,0:T(8,128)(2,1)} %bitcast.9, f32[1,256,768]{2,1,0:T(8,128)} %refs_2_.1, ...), custom_call_target="tpu_custom_call" | custom-call | tf_op jit(solution)/shard_map/block/pallas_call | solution.py:1119
  210.6 0.0 copy-start.1
  210.6 0.0 copy-start
  210.6 12.1 %adam.1 = (f32[256,768]{1,0:T(8,128)}, f32[256,256]{1,0:T(8,128)}, f32[256,1024]{1,0:T(8,128)}, f32[1024,256]{1,0:T(8,128)}, f32[1,256,768]{2,1,0:T(8,128)}, /*i...) custom-call(s32[4]{0:T(128)} %own_ref.3, ...), custom_call_target="tpu_custom_call" | custom-call | tf_op jit(solution)/shard_map/adam/pallas_call | solution.py:1264
  222.7 0.0 copy-done.1
  222.7 0.9 copy.52
  223.6 0.0 copy-done
  223.6 0.9 copy.53
Async XLA Ops:
  210.6 12.1 %copy-start.1 = (bf16[2,784,256]{2,1,0:T(8,128)(2,1)S(1)}, bf16[2,784,256]{2,1,0:T(8,128)(2,1)}, u32[]{:S(2)}) copy-start(bf16[2,784,256]{2,1,0:T(8,128)(2,1)} %get-tuple-element.47) | copy-start | bytes 2408452
  210.6 13.0 %copy-start = (bf16[2,784,256]{2,1,0:T(8,128)(2,1)S(1)}, bf16[2,784,256]{2,1,0:T(8,128)(2,1)}, u32[]{:S(2)}) copy-start(bf16[2,784,256]{2,1,0:T(8,128)(2,1)} %get-tuple-element.48) | copy-start | bytes 2408452
